TPU v7x, 32 devices: a whole 2x2x4 slice. The times are simulated.
32 devices in a mesh: dp: 8 (over z, x), seq: 4 (over y, core).
Axes of the slice: x: 2, y: 2, z: 4, core: 2. Of those that a mesh axis runs over, the one named last changes fastest.
Arguments:
- hidden_in: bfloat16 [8, 1024, 1024], P('dp', 'seq'), may hold values from -6 to 6
- segments: int32 [8, 1024], P('dp'), may hold values from 0 to 2, as said below
- cotangent: bfloat16 [8, 1024, 1024], P('dp', 'seq'), may hold values from -6 to 6
- in_proj: bfloat16 [1024, 3352], P(('dp', 'seq')), may hold values from -0.1875 to 0.1875
- query_proj: bfloat16 [1024, 512], P(('dp', 'seq')), may hold values from -0.1875 to 0.1875
- key_proj: bfloat16 [1024, 128], P(('dp', 'seq')), may hold values from -0.1875 to 0.1875
- value_proj: bfloat16 [1024, 128], P(('dp', 'seq')), may hold values from -0.1875 to 0.1875
- attn_proj: bfloat16 [512, 1024], P(('dp', 'seq')), may hold values from -4 to 4
- mixer_proj: bfloat16 [1536, 1024], P(('dp', 'seq')), may hold values from -0.15625 to 0.15625
- gate_proj: bfloat16 [1024, 2048], P(('dp', 'seq')), may hold values from -0.1875 to 0.1875
- up_proj: bfloat16 [1024, 2048], P(('dp', 'seq')), may hold values from -0.1875 to 0.1875
- down_proj: bfloat16 [2048, 1024], P(('dp', 'seq')), may hold values from -0.125 to 0.125
- conv_weight: bfloat16 [1792, 4], P(('dp', 'seq')), may hold values from -3 to 3
- conv_bias: bfloat16 [1792], P(('dp', 'seq')), may hold values from -1.5 to 1.5
- norm_one: bfloat16 [1024], P(('dp', 'seq')), may hold values from 0.5 to 1.5
- norm_two: bfloat16 [1024], P(('dp', 'seq')), may hold values from 0.5 to 1.5
- mixer_norm: bfloat16 [1536], P(('dp', 'seq')), may hold values from 0.5 to 1.5
- step_bias: float32 [24], replicated, may hold values from -3.5 to -2.5
- decay_log: float32 [24], replicated, may hold values from -6 to -1
- skip_gain: float32 [24], replicated, may hold values from 0.5 to 1.5
Outputs:
- layer_out: bfloat16 [8, 1024, 1024], P('dp', 'seq')
- input_grad: float32 [8, 1024, 1024], P('dp', 'seq')
- in_proj_grad: float32 [1024, 3352], P(('dp', 'seq'))
- query_proj_grad: float32 [1024, 512], P(('dp', 'seq'))
- key_proj_grad: float32 [1024, 128], P(('dp', 'seq'))
- value_proj_grad: float32 [1024, 128], P(('dp', 'seq'))
- attn_proj_grad: float32 [512, 1024], P(('dp', 'seq'))
- mixer_proj_grad: float32 [1536, 1024], P(('dp', 'seq'))
- gate_proj_grad: float32 [1024, 2048], P(('dp', 'seq'))
- up_proj_grad: float32 [1024, 2048], P(('dp', 'seq'))
- down_proj_grad: float32 [2048, 1024], P(('dp', 'seq'))
- conv_weight_grad: float32 [1792, 4], P(('dp', 'seq'))
- conv_bias_grad: float32 [1792], P(('dp', 'seq'))
- norm_one_grad: float32 [1024], P(('dp', 'seq'))
- norm_two_grad: float32 [1024], P(('dp', 'seq'))
- mixer_norm_grad: float32 [1536], P(('dp', 'seq'))
- step_bias_grad: float32 [24], replicated
- decay_log_grad: float32 [24], replicated
- skip_gain_grad: float32 [24], replicated
Inputs may be any that keep to these rules, and one draw needn't show every extreme that they name: Each sequence holds segments 0, 1 and 2 in order; segment 1 begins within the first half of 256 positions, segment 2 within the last half of 256 positions.
All inputs are finite; a program needn't handle non-finite values.
Results may differ from a plain program's by a relative error of at most 0.02.
Values may be sent and summed in bfloat16 or wider, within the bound.
A program may use at most 96 MiB of HBM per device.

v0:
```python
import jax
import jax.numpy as jnp
from jax import lax
from jax.sharding import PartitionSpec as P

H = 24
P_SIZE = 64
N = 128
CONV = 4
NH = 8
KVH = 2
HD = 64


epsilon = 1e-05
highest = lax.Precision.HIGHEST


def passed_along(shard, axis, by):
    size = lax.axis_size(axis)
    pairs = [(i, i + by) for i in range(size) if 0 <= i + by < size]
    return lax.ppermute(shard, axis, pairs)


def carried_in_2(shard, axis, combine, identity):
    size, here = (lax.axis_size(axis), lax.axis_index(axis))
    everything = jax.tree.map(
        lambda part, kind: lax.all_gather(part.astype(kind), axis),
        shard,
        (jnp.bfloat16, jnp.bfloat16),
    )
    start = jax.tree.map(
        lambda part, zero: jnp.broadcast_to(jnp.asarray(zero, part.dtype), part.shape),
        shard,
        identity,
    )

    def carried_lap(k, before):
        reached = k < here
        new = combine(
            before, jax.tree.map(lambda part, own: part[k].astype(own.dtype), everything, shard)
        )
        return jax.tree.map(lambda a, b: jnp.where(reached, a, b), new, before)

    return lax.fori_loop(0, size, carried_lap, start)


def entering(shard, axis, combine, identity):
    size, here = (lax.axis_size(axis), lax.axis_index(axis))
    everything = jax.tree.map(
        lambda part, kind: lax.all_gather(part.astype(kind), axis),
        shard,
        jax.tree.map(lambda a: jnp.bfloat16 if a.dtype == jnp.float32 else a.dtype, shard),
    )
    start = jax.tree.map(
        lambda part, zero: jnp.broadcast_to(jnp.asarray(zero, part.dtype), part.shape),
        shard,
        identity,
    )

    def entering_lap(k, before):
        at = size - 1 - k
        reached = at > here
        new = combine(
            before, jax.tree.map(lambda part, own: part[at].astype(own.dtype), everything, shard)
        )
        return jax.tree.map(lambda a, b: jnp.where(reached, a, b), new, before)

    return lax.fori_loop(0, size, entering_lap, start)


def rms_scale(values, gain_vec):
    return (
        values * lax.rsqrt(jnp.mean(values * values, axis=-1, keepdims=True) + epsilon) * gain_vec
    )


def product(left_side, right_side):
    return jnp.dot(left_side, right_side, preferred_element_type=jnp.float32)


def weight_sum(left_side, right_side):
    return jnp.einsum("std,ste->de", left_side, right_side, preferred_element_type=jnp.float32)


def back_product(grad_rows, weight):
    return jnp.einsum("ste,de->std", grad_rows, weight, preferred_element_type=jnp.float32)


def join_forward(earlier, later):
    return (earlier[0] * later[0], later[0][:, :, None, None] * earlier[1] + later[1])


def join_backward(earlier, later):
    return (later[0] * earlier[0], later[1] + later[0][:, :, None, None] * earlier[1])


def conv_part(extended, step_raw, conv_weight, conv_bias, step_bias, decay_log, tap_masks):
    rows_here = step_raw.shape[1]
    running = conv_bias
    for offset in range(CONV):
        running = (
            running
            + conv_weight[:, offset]
            * extended[:, offset : offset + rows_here]
            * tap_masks[offset][:, :, None]
        )
    conv_out = jax.nn.silu(running)
    head_input = conv_out[..., : H * P_SIZE].reshape(conv_out.shape[0], rows_here, H, P_SIZE)
    write_vec = conv_out[..., H * P_SIZE : H * P_SIZE + N]
    read_vec = conv_out[..., H * P_SIZE + N :]
    step_size = jax.nn.softplus(step_raw + step_bias)
    log_decay = jnp.cumsum(step_size * -jnp.exp(decay_log), axis=1)
    return (head_input, write_vec, read_vec, step_size, log_decay)


def state_part(head_input, write_vec, step_size, log_decay, to_end, across):
    gap_end = log_decay[:, -1:, :] - log_decay
    weight_end = jnp.exp(gap_end) * to_end[:, :, None] * step_size
    state_local = jnp.einsum(
        "sth,sthp,stn->shpn", weight_end, head_input, write_vec, precision=highest
    )
    block_decay = jnp.exp(log_decay[:, -1, :]) * across[:, None]
    return (block_decay, state_local)


def output_part(
    head_input,
    write_vec,
    read_vec,
    step_size,
    log_decay,
    gate_z,
    skip_gain,
    mixer_gain,
    state_in,
    allowed,
    from_before,
):
    log_gap = jnp.where(
        allowed[..., None], log_decay[:, :, None, :] - log_decay[:, None, :, :], -10000.0
    )
    inner_prod = jnp.einsum("stn,sun->stu", read_vec, write_vec, precision=highest)
    mixing = jnp.exp(log_gap) * inner_prod[..., None] * step_size[:, None, :, :]
    result = jnp.einsum("stuh,suhp->sthp", mixing, head_input, precision=highest)
    carried = jnp.exp(log_decay) * from_before[:, :, None]
    result = result + carried[..., None] * jnp.einsum(
        "stn,shpn->sthp", read_vec, state_in, precision=highest
    )
    result = result + skip_gain[:, None] * head_input
    gated = result.reshape(gate_z.shape) * jax.nn.silu(gate_z)
    return rms_scale(gated, mixer_gain)


def attention_scores(query, all_keys, allowed_keys):
    seqs_here, rows_here = (query.shape[0], query.shape[1])
    group_size = NH // KVH
    query_heads = query.reshape(seqs_here, rows_here, KVH, group_size, HD)
    key_heads = all_keys.reshape(seqs_here, all_keys.shape[1], KVH, HD)
    scores = jnp.einsum(
        "stkgd,sukd->skgtu", query_heads, key_heads, preferred_element_type=jnp.float32
    ) * HD ** (-0.5)
    return jnp.where(allowed_keys[:, None, None], scores, -1e30)


def body(
    hidden_in,
    segments,
    cotangent,
    in_proj,
    query_proj,
    key_proj,
    value_proj,
    attn_proj,
    mixer_proj,
    gate_proj,
    up_proj,
    down_proj,
    conv_weight,
    conv_bias,
    norm_one,
    norm_two,
    mixer_norm,
    step_bias,
    decay_log,
    skip_gain,
):
    (
        full_in,
        full_query,
        full_key,
        full_value,
        full_attn,
        full_mixer,
        full_gate,
        full_up,
        full_down,
        full_conv,
        full_bias,
        full_one,
        full_two,
        full_gain,
    ) = (
        lax.all_gather(in_proj, ("dp", "seq"), axis=0, tiled=True),
        lax.all_gather(query_proj, ("dp", "seq"), axis=0, tiled=True),
        lax.all_gather(key_proj, ("dp", "seq"), axis=0, tiled=True),
        lax.all_gather(value_proj, ("dp", "seq"), axis=0, tiled=True),
        lax.all_gather(attn_proj, ("dp", "seq"), axis=0, tiled=True),
        lax.all_gather(mixer_proj, ("dp", "seq"), axis=0, tiled=True),
        lax.all_gather(gate_proj, ("dp", "seq"), axis=0, tiled=True),
        lax.all_gather(up_proj, ("dp", "seq"), axis=0, tiled=True),
        lax.all_gather(down_proj, ("dp", "seq"), axis=0, tiled=True),
        lax.all_gather(conv_weight, ("dp", "seq"), axis=0, tiled=True),
        lax.all_gather(conv_bias, ("dp", "seq"), axis=0, tiled=True),
        lax.all_gather(norm_one, ("dp", "seq"), axis=0, tiled=True),
        lax.all_gather(norm_two, ("dp", "seq"), axis=0, tiled=True),
        lax.all_gather(mixer_norm, ("dp", "seq"), axis=0, tiled=True),
    )
    seqs_here, rows_here = (hidden_in.shape[0], hidden_in.shape[1])
    seq_length = segments.shape[1]
    first_row = lax.axis_index("seq") * rows_here
    group_size = NH // KVH
    inner_width = H * P_SIZE
    conv_width = H * P_SIZE + 2 * N
    padded_ids = jnp.concatenate([jnp.full((seqs_here, CONV - 1), -1, jnp.int32), segments], axis=1)
    ext_ids = lax.dynamic_slice_in_dim(padded_ids, first_row, rows_here + CONV - 1, 1)
    here_ids = ext_ids[:, CONV - 1 :]
    before_id = ext_ids[:, CONV - 2]
    tap_masks = [
        (ext_ids[:, offset : offset + rows_here] == here_ids).astype(jnp.float32)
        for offset in range(CONV)
    ]
    local_pos = jnp.arange(rows_here)
    allowed = (here_ids[:, :, None] == here_ids[:, None, :]) & (
        local_pos[:, None] >= local_pos[None, :]
    )
    to_end = (here_ids == here_ids[:, -1:]).astype(jnp.float32)
    from_before = (here_ids == before_id[:, None]).astype(jnp.float32)
    across = (here_ids[:, -1] == before_id).astype(jnp.float32)
    query_pos = first_row + local_pos
    key_pos = jnp.arange(seq_length)
    allowed_keys = (here_ids[:, :, None] == segments[:, None, :]) & (
        query_pos[:, None] >= key_pos[None, :]
    )
    hidden_f = hidden_in.astype(jnp.float32)
    gain_one = full_one.astype(jnp.float32)
    gain_two = full_two.astype(jnp.float32)
    mixer_gain = full_gain.astype(jnp.float32)
    normed = rms_scale(hidden_f, gain_one).astype(jnp.bfloat16)
    projected = product(normed, full_in).astype(jnp.bfloat16)
    query = product(normed, full_query).astype(jnp.bfloat16)
    keys_own = product(normed, full_key).astype(jnp.bfloat16)
    values_own = product(normed, full_value).astype(jnp.bfloat16)
    all_keys, all_values = (
        lax.all_gather(keys_own, "seq", axis=1, tiled=True),
        lax.all_gather(values_own, "seq", axis=1, tiled=True),
    )
    rim_rows = passed_along(
        projected[:, rows_here - CONV + 1 :, inner_width : inner_width + conv_width], "seq", 1
    )
    extended = jnp.concatenate(
        [rim_rows, projected[:, :, inner_width : inner_width + conv_width]], axis=1
    ).astype(jnp.float32)
    gate_z = projected[..., :inner_width].astype(jnp.float32)
    step_raw = projected[..., inner_width + conv_width :].astype(jnp.float32)
    conv_inputs = (
        extended,
        step_raw,
        full_conv.astype(jnp.float32),
        full_bias.astype(jnp.float32),
        step_bias,
        decay_log,
    )

    def conv_fn(ext_in, raw_in, weight_in, bias_in, step_in, decay_in):
        return conv_part(ext_in, raw_in, weight_in, bias_in, step_in, decay_in, tap_masks)

    def state_fn(head_input, write_vec, step_size, log_decay):
        return state_part(head_input, write_vec, step_size, log_decay, to_end, across)

    def output_fn(
        head_input, write_vec, read_vec, step_size, log_decay, gate_in, skip_in, gain_in, state_in
    ):
        return output_part(
            head_input,
            write_vec,
            read_vec,
            step_size,
            log_decay,
            gate_in,
            skip_in,
            gain_in,
            state_in,
            allowed,
            from_before,
        )

    head_input, write_vec, read_vec, step_size, log_decay = conv_fn(*conv_inputs)
    block_decay, state_local = state_fn(head_input, write_vec, step_size, log_decay)
    carried_in = carried_in_2(
        (block_decay, state_local),
        "seq",
        join_forward,
        (jnp.ones_like(block_decay), jnp.zeros_like(state_local)),
    )
    state_in = carried_in[1]
    output_inputs = (
        head_input,
        write_vec,
        read_vec,
        step_size,
        log_decay,
        gate_z,
        skip_gain,
        mixer_gain,
        state_in,
    )
    mixed = output_fn(*output_inputs).astype(jnp.bfloat16)
    mixer_out = product(mixed, full_mixer)
    scores = attention_scores(query, all_keys, allowed_keys)
    row_max = jnp.max(scores, axis=-1, keepdims=True)
    log_total = row_max + jnp.log(jnp.sum(jnp.exp(scores - row_max), axis=-1, keepdims=True))
    attn_probs = jnp.exp(scores - log_total).astype(jnp.bfloat16)
    value_heads = all_values.reshape(seqs_here, seq_length, KVH, HD)
    attn_mix = jnp.einsum(
        "skgtu,sukd->stkgd", attn_probs, value_heads, preferred_element_type=jnp.float32
    )
    attn_mix = attn_mix.reshape(seqs_here, rows_here, NH * HD).astype(jnp.bfloat16)
    attn_out = product(attn_mix, full_attn)
    resid = hidden_f + mixer_out + attn_out
    normed_two = rms_scale(resid, gain_two).astype(jnp.bfloat16)
    gate_val = product(normed_two, full_gate)
    up_val = product(normed_two, full_up)
    sigmoid_gate = jax.nn.sigmoid(gate_val)
    activated = (gate_val * sigmoid_gate * up_val).astype(jnp.bfloat16)
    layer_out = (resid + product(activated, full_down)).astype(jnp.bfloat16)
    (
        full_in,
        full_query,
        full_key,
        full_value,
        full_attn,
        full_mixer,
        full_gate,
        full_up,
        full_down,
    ) = (
        lax.all_gather(in_proj, ("dp", "seq"), axis=0, tiled=True),
        lax.all_gather(query_proj, ("dp", "seq"), axis=0, tiled=True),
        lax.all_gather(key_proj, ("dp", "seq"), axis=0, tiled=True),
        lax.all_gather(value_proj, ("dp", "seq"), axis=0, tiled=True),
        lax.all_gather(attn_proj, ("dp", "seq"), axis=0, tiled=True),
        lax.all_gather(mixer_proj, ("dp", "seq"), axis=0, tiled=True),
        lax.all_gather(gate_proj, ("dp", "seq"), axis=0, tiled=True),
        lax.all_gather(up_proj, ("dp", "seq"), axis=0, tiled=True),
        lax.all_gather(down_proj, ("dp", "seq"), axis=0, tiled=True),
    )
    grad_top = cotangent.astype(jnp.float32)
    down_w_grad = jnp.einsum(
        "sti,std->id", activated, cotangent, preferred_element_type=jnp.float32
    )
    act_grad = back_product(cotangent, full_down)
    gate_grad = (act_grad * up_val * sigmoid_gate * (1.0 + gate_val * (1.0 - sigmoid_gate))).astype(
        jnp.bfloat16
    )
    up_grad = (act_grad * gate_val * sigmoid_gate).astype(jnp.bfloat16)
    gate_w_grad = weight_sum(normed_two, gate_grad)
    up_w_grad = weight_sum(normed_two, up_grad)
    normed_two_grad = back_product(gate_grad, full_gate) + back_product(up_grad, full_up)
    resid_part, two_grad = jax.vjp(rms_scale, resid, gain_two)[1](normed_two_grad)
    resid_grad = grad_top + resid_part
    resid_low = resid_grad.astype(jnp.bfloat16)
    attn_w_grad = weight_sum(attn_mix, resid_low)
    mixer_w_grad = weight_sum(mixed, resid_low)
    mix_grad = back_product(resid_low, full_attn).astype(jnp.bfloat16)
    mixed_grad = back_product(resid_low, full_mixer)
    probs_full = jnp.exp(attention_scores(query, all_keys, allowed_keys) - log_total)
    mix_heads = mix_grad.reshape(seqs_here, rows_here, KVH, group_size, HD)
    probs_grad = jnp.einsum(
        "stkgd,sukd->skgtu", mix_heads, value_heads, preferred_element_type=jnp.float32
    )
    score_grad = (
        probs_full * (probs_grad - jnp.sum(probs_full * probs_grad, axis=-1, keepdims=True))
    ).astype(jnp.bfloat16)
    key_heads = all_keys.reshape(seqs_here, seq_length, KVH, HD)
    query_heads = query.reshape(seqs_here, rows_here, KVH, group_size, HD)
    query_grad = jnp.einsum(
        "skgtu,sukd->stkgd", score_grad, key_heads, preferred_element_type=jnp.float32
    ) * HD ** (-0.5)
    query_grad = query_grad.reshape(seqs_here, rows_here, NH * HD).astype(jnp.bfloat16)
    key_part = jnp.einsum(
        "skgtu,stkgd->sukd", score_grad, query_heads, preferred_element_type=jnp.float32
    ) * HD ** (-0.5)
    value_part = jnp.einsum(
        "skgtu,stkgd->sukd", attn_probs, mix_heads, preferred_element_type=jnp.float32
    )
    key_sum, value_sum = (
        lax.psum_scatter(
            key_part.reshape(seqs_here, seq_length, KVH * HD).astype(jnp.bfloat16),
            "seq",
            scatter_dimension=1,
            tiled=True,
        ).astype(jnp.float32),
        lax.psum_scatter(
            value_part.reshape(seqs_here, seq_length, KVH * HD).astype(jnp.bfloat16),
            "seq",
            scatter_dimension=1,
            tiled=True,
        ).astype(jnp.float32),
    )
    key_grad = key_sum.astype(jnp.bfloat16)
    value_grad = value_sum.astype(jnp.bfloat16)
    (
        input_a,
        write_a,
        read_a,
        step_a,
        decay_a,
        gate_z_grad,
        skip_grad,
        mixer_gain_grad,
        state_grad,
    ) = jax.vjp(output_fn, *output_inputs)[1](mixed_grad)
    passed_back = entering(
        (block_decay, state_grad),
        "seq",
        join_backward,
        (jnp.ones_like(block_decay), jnp.zeros_like(state_grad)),
    )
    later_grad = passed_back[1]
    block_grad = jnp.sum(later_grad * state_in, axis=(2, 3))
    input_b, write_b, step_b, decay_b = jax.vjp(
        state_fn, head_input, write_vec, step_size, log_decay
    )[1]((block_grad, later_grad))
    ext_grad, raw_grad, conv_w_grad, conv_b_grad, step_bias_grad, decay_log_grad = jax.vjp(
        conv_fn, *conv_inputs
    )[1]((input_a + input_b, write_a + write_b, read_a, step_a + step_b, decay_a + decay_b))
    rim_grad = passed_along(ext_grad[:, : CONV - 1], "seq", -1)
    conv_in_grad = ext_grad[:, CONV - 1 :] + jnp.concatenate(
        [jnp.zeros((seqs_here, rows_here - CONV + 1, conv_width), jnp.float32), rim_grad], axis=1
    )
    proj_grad = jnp.concatenate([gate_z_grad, conv_in_grad, raw_grad], axis=-1).astype(jnp.bfloat16)
    in_w_grad = weight_sum(normed, proj_grad)
    query_w_grad = weight_sum(normed, query_grad)
    key_w_grad = weight_sum(normed, key_grad)
    value_w_grad = weight_sum(normed, value_grad)
    normed_grad = (
        back_product(proj_grad, full_in)
        + back_product(query_grad, full_query)
        + back_product(key_grad, full_key)
        + back_product(value_grad, full_value)
    )
    input_part, one_grad = jax.vjp(rms_scale, hidden_f, gain_one)[1](normed_grad)
    input_grad = resid_grad + input_part
    shares = (
        lax.psum_scatter(
            in_w_grad.astype(jnp.bfloat16), "dp", scatter_dimension=0, tiled=True
        ).astype(jnp.float32),
        lax.psum_scatter(
            query_w_grad.astype(jnp.bfloat16), "dp", scatter_dimension=0, tiled=True
        ).astype(jnp.float32),
        lax.psum_scatter(
            key_w_grad.astype(jnp.bfloat16), "dp", scatter_dimension=0, tiled=True
        ).astype(jnp.float32),
        lax.psum_scatter(
            value_w_grad.astype(jnp.bfloat16), "dp", scatter_dimension=0, tiled=True
        ).astype(jnp.float32),
        lax.psum_scatter(
            attn_w_grad.astype(jnp.bfloat16), "dp", scatter_dimension=0, tiled=True
        ).astype(jnp.float32),
        lax.psum_scatter(
            mixer_w_grad.astype(jnp.bfloat16), "dp", scatter_dimension=0, tiled=True
        ).astype(jnp.float32),
        lax.psum_scatter(
            gate_w_grad.astype(jnp.bfloat16), "dp", scatter_dimension=0, tiled=True
        ).astype(jnp.float32),
        lax.psum_scatter(
            up_w_grad.astype(jnp.bfloat16), "dp", scatter_dimension=0, tiled=True
        ).astype(jnp.float32),
        lax.psum_scatter(
            down_w_grad.astype(jnp.bfloat16), "dp", scatter_dimension=0, tiled=True
        ).astype(jnp.float32),
        lax.psum_scatter(
            conv_w_grad.astype(jnp.bfloat16), "dp", scatter_dimension=0, tiled=True
        ).astype(jnp.float32),
        lax.psum_scatter(
            conv_b_grad.astype(jnp.bfloat16), "dp", scatter_dimension=0, tiled=True
        ).astype(jnp.float32),
        lax.psum_scatter(
            one_grad.astype(jnp.bfloat16), "dp", scatter_dimension=0, tiled=True
        ).astype(jnp.float32),
        lax.psum_scatter(
            two_grad.astype(jnp.bfloat16), "dp", scatter_dimension=0, tiled=True
        ).astype(jnp.float32),
        lax.psum_scatter(
            mixer_gain_grad.astype(jnp.bfloat16), "dp", scatter_dimension=0, tiled=True
        ).astype(jnp.float32),
    )
    owned = (
        lax.psum_scatter(
            shares[0].astype(jnp.bfloat16), "seq", scatter_dimension=0, tiled=True
        ).astype(jnp.float32),
        lax.psum_scatter(
            shares[1].astype(jnp.bfloat16), "seq", scatter_dimension=0, tiled=True
        ).astype(jnp.float32),
        lax.psum_scatter(
            shares[2].astype(jnp.bfloat16), "seq", scatter_dimension=0, tiled=True
        ).astype(jnp.float32),
        lax.psum_scatter(
            shares[3].astype(jnp.bfloat16), "seq", scatter_dimension=0, tiled=True
        ).astype(jnp.float32),
        lax.psum_scatter(
            shares[4].astype(jnp.bfloat16), "seq", scatter_dimension=0, tiled=True
        ).astype(jnp.float32),
        lax.psum_scatter(
            shares[5].astype(jnp.bfloat16), "seq", scatter_dimension=0, tiled=True
        ).astype(jnp.float32),
        lax.psum_scatter(
            shares[6].astype(jnp.bfloat16), "seq", scatter_dimension=0, tiled=True
        ).astype(jnp.float32),
        lax.psum_scatter(
            shares[7].astype(jnp.bfloat16), "seq", scatter_dimension=0, tiled=True
        ).astype(jnp.float32),
        lax.psum_scatter(
            shares[8].astype(jnp.bfloat16), "seq", scatter_dimension=0, tiled=True
        ).astype(jnp.float32),
        lax.psum_scatter(
            shares[9].astype(jnp.bfloat16), "seq", scatter_dimension=0, tiled=True
        ).astype(jnp.float32),
        lax.psum_scatter(
            shares[10].astype(jnp.bfloat16), "seq", scatter_dimension=0, tiled=True
        ).astype(jnp.float32),
        lax.psum_scatter(
            shares[11].astype(jnp.bfloat16), "seq", scatter_dimension=0, tiled=True
        ).astype(jnp.float32),
        lax.psum_scatter(
            shares[12].astype(jnp.bfloat16), "seq", scatter_dimension=0, tiled=True
        ).astype(jnp.float32),
        lax.psum_scatter(
            shares[13].astype(jnp.bfloat16), "seq", scatter_dimension=0, tiled=True
        ).astype(jnp.float32),
    )
    head_sums = lax.psum((step_bias_grad, decay_log_grad, skip_grad), ("dp", "seq"))
    return (
        layer_out,
        input_grad,
        owned[0],
        owned[1],
        owned[2],
        owned[3],
        owned[4],
        owned[5],
        owned[6],
        owned[7],
        owned[8],
        owned[9],
        owned[10],
        owned[11],
        owned[12],
        owned[13],
        head_sums[0],
        head_sums[1],
        head_sums[2],
    )


def solution(mesh):
    placed = (
        P("dp", "seq", None),
        P("dp", None),
        P("dp", "seq", None),
        P(("dp", "seq"), None),
        P(("dp", "seq"), None),
        P(("dp", "seq"), None),
        P(("dp", "seq"), None),
        P(("dp", "seq"), None),
        P(("dp", "seq"), None),
        P(("dp", "seq"), None),
        P(("dp", "seq"), None),
        P(("dp", "seq"), None),
        P(("dp", "seq"), None),
        P(("dp", "seq")),
        P(("dp", "seq")),
        P(("dp", "seq")),
        P(("dp", "seq")),
        P(),
        P(),
        P(),
    )
    return jax.shard_map(
        body,
        mesh=mesh,
        in_specs=placed,
        out_specs=(
            P("dp", "seq", None),
            P("dp", "seq", None),
            P(("dp", "seq"), None),
            P(("dp", "seq"), None),
            P(("dp", "seq"), None),
            P(("dp", "seq"), None),
            P(("dp", "seq"), None),
            P(("dp", "seq"), None),
            P(("dp", "seq"), None),
            P(("dp", "seq"), None),
            P(("dp", "seq"), None),
            P(("dp", "seq"), None),
            P(("dp", "seq")),
            P(("dp", "seq")),
            P(("dp", "seq")),
            P(("dp", "seq")),
            P(),
            P(),
            P(),
        ),
        check_vma=False,
    )
```

profile of v0, /device:TPU:0, one launch (start us, length us, event | category | flops | bytes accessed | tf_op | source)
XLA Modules:
  0.0 1595.4 jit_solution(8080279827595548398)
XLA Ops:
  12.8 42.4 %all-reduce.29 = (bf16[1024]{0:T(1024)(128)(2,1)S(1)}, bf16[1792]{0:T(1024)(128)(2,1)S(1)}, bf16[1536]{0:T(1024)(128)(2,1)}, bf16[1024]{0:T(1024)(128)(2,1)}) all-reduce(bf16[1024]{0:T(1024)(128)(2,1)S(1)} %dynamic-update-slice.1, bf16[1792]{0:T(1024)(128)(2,1)S(1)} %dynamic-update-slice, ...), channel_id=1, replica_groups=mesh['dp'=8,'seq'=4] {'dp','seq'}, use_global_device_ids=true, to_apply=%add.16 | all-reduce | flops 5376 | bytes 21504
  57.1 41.5 %all-gather.4 = bf16[32,56,4]{1,2,0:T(4,128)(2,1)S(1)} all-gather(bf16[1,56,4]{1,2,0:T(4,128)(2,1)} %bitcast.559), channel_id=1, replica_groups=mesh['dp'=8,'seq'=4] {'dp','seq'}, dimensions={0}, use_global_device_ids=true | all-gather | bytes 14784 | tf_op jit(solution)/shard_map/all_gather | solution.py:213
  130.2 37.4 %all_gather.86 = bf16[1024,128]{1,0:T(8,128)(2,1)S(1)} all-gather(bf16[32,128]{1,0:T(8,128)(2,1)S(1)} %copy-done.115), channel_id=1, replica_groups=mesh['dp'=8,'seq'=4] {'dp','seq'}, dimensions={0}, use_global_device_ids=true | all-gather | bytes 270336 | tf_op jit(solution)/shard_map/all_gather | solution.py:206
  176.7 39.0 %all_gather.84 = bf16[1024,128]{1,0:T(8,128)(2,1)S(1)} all-gather(bf16[32,128]{1,0:T(8,128)(2,1)S(1)} %copy-done.116), channel_id=1, replica_groups=mesh['dp'=8,'seq'=4] {'dp','seq'}, dimensions={0}, use_global_device_ids=true | all-gather | bytes 270336 | tf_op jit(solution)/shard_map/all_gather | solution.py:207
  268.1 13.2 all-gather.17.cloned.1.call-done
  286.9 58.0 %all-gather.23.cloned.1.call-done = bf16[1024,2048]{1,0:T(8,128)(2,1)} async-done(((bf16[32,2048]{1,0:T(8,128)(2,1)}), bf16[1024,2048]{1,0:T(8,128)(2,1)}) %all-gather.23.cloned.1.call-update) | async-done | bytes 4194320 | tf_op jit(solution)/shard_map/all_gather | solution.py:210
  349.8 58.6 %all-gather.25.cloned.1.call-done = bf16[1024,2048]{1,0:T(8,128)(2,1)} async-done(((bf16[32,2048]{1,0:T(8,128)(2,1)}), bf16[1024,2048]{1,0:T(8,128)(2,1)}) %all-gather.25.cloned.1.call-update) | async-done | bytes 4194320 | tf_op jit(solution)/shard_map/all_gather | solution.py:211
  413.3 58.6 %all-gather.27.cloned.1.call-done = bf16[2048,1024]{1,0:T(8,128)(2,1)} async-done(((bf16[64,1024]{1,0:T(8,128)(2,1)}), bf16[2048,1024]{1,0:T(8,128)(2,1)}) %all-gather.27.cloned.1.call-update) | async-done | bytes 4194320 | tf_op jit(solution)/shard_map/all_gather | solution.py:212
  488.8 9.8 fusion.2
  514.5 9.3 reduce-scatter.31.cloned.1.call-done
  526.0 20.9 %reduce-scatter.29.cloned.1.call-done = bf16[1,256,128]{1,2,0:T(8,128)(2,1)} async-done(((bf16[1,1024,128]{1,2,0:T(8,128)(2,1)}), bf16[1,256,128]{1,2,0:T(8,128)(2,1)}) %reduce-scatter.29.cloned.1.call-update) | async-done | bytes 65552 | tf_op jit(solution)/shard_map/reduce_scatter | solution.py:398
  599.0 12.4 reduce-scatter.41.cloned.1.call-done
  611.6 12.1 fusion.14
  623.7 51.8 %reduce-scatter.37.cloned.1.call-done = bf16[128,128]{1,0:T(8,128)(2,1)} async-done(((bf16[1024,128]{1,0:T(8,128)(2,1)}), bf16[128,128]{1,0:T(8,128)(2,1)}) %reduce-scatter.37.cloned.1.call-update) | async-done | bytes 32784 | tf_op jit(solution)/shard_map/reduce_scatter | solution.py:462
  677.8 63.7 %reduce-scatter.33.cloned.1.call-done = bf16[128,512]{1,0:T(8,128)(2,1)} async-done(((bf16[1024,512]{1,0:T(8,128)(2,1)}), bf16[128,512]{1,0:T(8,128)(2,1)}) %reduce-scatter.33.cloned.1.call-update) | async-done | bytes 131088 | tf_op jit(solution)/shard_map/reduce_scatter | solution.py:459
  755.8 51.9 %reduce-scatter.45.cloned.1.call-done = bf16[64,1024]{1,0:T(8,128)(2,1)} async-done(((bf16[512,1024]{1,0:T(8,128)(2,1)}), bf16[64,1024]{1,0:T(8,128)(2,1)}) %reduce-scatter.45.cloned.1.call-update) | async-done | bytes 131088 | tf_op jit(solution)/shard_map/reduce_scatter | solution.py:468
  808.2 20.2 %all-gather.31.cloned.1.call-done = bf16[96,64,128]{2,1,0:T(8,128)(2,1)} async-done(((bf16[24,64,128]{2,1,0:T(8,128)(2,1)}), bf16[96,64,128]{2,1,0:T(8,128)(2,1)}) %all-gather.31.cloned.1.call-update) | async-done | bytes 1572880 | tf_op jit(solution)/shard_map/all_gather | solution.py:51
  873.9 9.6 copy.302
  885.4 20.8 %reduce-scatter.49.cloned.1.call-done = bf16[192,1024]{1,0:T(8,128)(2,1)} async-done(((bf16[1536,1024]{1,0:T(8,128)(2,1)}), bf16[192,1024]{1,0:T(8,128)(2,1)}) %reduce-scatter.49.cloned.1.call-update) | async-done | bytes 393232 | tf_op jit(solution)/shard_map/reduce_scatter | solution.py:471
  906.3 90.5 %reduce-scatter.53.cloned.1.call-done = bf16[128,2048]{1,0:T(8,128)(2,1)} async-done(((bf16[1024,2048]{1,0:T(8,128)(2,1)}), bf16[128,2048]{1,0:T(8,128)(2,1)}) %reduce-scatter.53.cloned.1.call-update) | async-done | bytes 524304 | tf_op jit(solution)/shard_map/reduce_scatter | solution.py:474
  996.8 91.6 %reduce-scatter.57.cloned.1.call-done = bf16[128,2048]{1,0:T(8,128)(2,1)} async-done(((bf16[1024,2048]{1,0:T(8,128)(2,1)}), bf16[128,2048]{1,0:T(8,128)(2,1)}) %reduce-scatter.57.cloned.1.call-update) | async-done | bytes 524304 | tf_op jit(solution)/shard_map/reduce_scatter | solution.py:477
  1088.5 91.4 %reduce-scatter.61.cloned.1.call-done = bf16[256,1024]{1,0:T(8,128)(2,1)} async-done(((bf16[2048,1024]{1,0:T(8,128)(2,1)}), bf16[256,1024]{1,0:T(8,128)(2,1)}) %reduce-scatter.61.cloned.1.call-update) | async-done | bytes 524304 | tf_op jit(solution)/shard_map/reduce_scatter | solution.py:480
  1202.7 20.5 %reduce-scatter.39.cloned.1.call-done = bf16[32,128]{1,0:T(8,128)(2,1)} async-done(((bf16[128,128]{1,0:T(8,128)(2,1)}), bf16[32,128]{1,0:T(8,128)(2,1)}) %reduce-scatter.39.cloned.1.call-update) | async-done | bytes 8208 | tf_op jit(solution)/shard_map/reduce_scatter | solution.py:506
  1224.5 39.4 %all-reduce.28 = (f32[24]{0:T(128)}, f32[24]{0:T(128)}, f32[24]{0:T(128)}) all-reduce(f32[24]{0:T(128)S(1)} %get-tuple-element.543, f32[24]{0:T(128)S(1)} %negate_multiply_fusion, f32[24]{0:T(128)S(1)} %reduce_sum.293), channel_id=1, replica_groups=mesh['dp'=8,'seq'=4] {'dp','seq'}, use_global_device_ids=true, to_apply=%region_63.64 | all-reduce | flops 72 | bytes 576 | tf_op jit(solution)/shard_map/psum | solution.py:543
  1268.8 131.7 %reduce-scatter.65.cloned.1.call-done = bf16[128,3352]{1,0:T(8,128)(2,1)} async-done(((bf16[1024,3352]{1,0:T(8,128)(2,1)}), bf16[128,3352]{1,0:T(8,128)(2,1)}) %reduce-scatter.65.cloned.1.call-update) | async-done | bytes 858128
  1408.8 35.3 %all-reduce.30 = (bf16[1792]{0:T(1024)(128)(2,1)S(1)}, bf16[1024]{0:T(1024)(128)(2,1)S(1)}, bf16[1024]{0:T(1024)(128)(2,1)S(1)}, bf16[1536]{0:T(1024)(128)(2,1)S(1)}) all-reduce(bf16[1792]{0:T(1024)(128)(2,1)S(1)} %copy-done.93, bf16[1024]{0:T(1024)(128)(2,1)S(1)} %get-tuple-element.499, ...), channel_id=28, replica_groups=mesh['dp'=8,'seq'=4] {'dp'}, use_global_device_ids=true, to_apply=%region_51.52.clone | all-reduce | flops 5376 | bytes 21504
  1447.3 17.3 %reduce-scatter.69.cloned.1.call-done = bf16[224,4]{1,0:T(8,128)(2,1)} async-done(((bf16[1792,4]{1,0:T(8,128)(2,1)}), bf16[224,4]{1,0:T(8,128)(2,1)}) %reduce-scatter.69.cloned.1.call-update) | async-done | bytes 1808
  1473.6 13.4 reduce-scatter.51.cloned.1.call-done
  1488.5 22.6 %reduce-scatter.55.cloned.1.call-done = bf16[32,2048]{1,0:T(8,128)(2,1)} async-done(((bf16[128,2048]{1,0:T(8,128)(2,1)}), bf16[32,2048]{1,0:T(8,128)(2,1)}) %reduce-scatter.55.cloned.1.call-update) | async-done | bytes 131088 | tf_op jit(solution)/shard_map/reduce_scatter | solution.py:518
  1512.8 22.5 %reduce-scatter.59.cloned.1.call-done = bf16[32,2048]{1,0:T(8,128)(2,1)} async-done(((bf16[128,2048]{1,0:T(8,128)(2,1)}), bf16[32,2048]{1,0:T(8,128)(2,1)}) %reduce-scatter.59.cloned.1.call-update) | async-done | bytes 131088 | tf_op jit(solution)/shard_map/reduce_scatter | solution.py:521
  1536.9 22.7 %reduce-scatter.63.cloned.1.call-done = bf16[64,1024]{1,0:T(8,128)(2,1)} async-done(((bf16[256,1024]{1,0:T(8,128)(2,1)}), bf16[64,1024]{1,0:T(8,128)(2,1)}) %reduce-scatter.63.cloned.1.call-update) | async-done | bytes 131088 | tf_op jit(solution)/shard_map/reduce_scatter | solution.py:524
  1561.3 24.7 %reduce-scatter.67.cloned.1.call-done = bf16[32,3352]{1,0:T(8,128)(2,1)} async-done(((bf16[128,3352]{1,0:T(8,128)(2,1)}), bf16[32,3352]{1,0:T(8,128)(2,1)}) %reduce-scatter.67.cloned.1.call-update) | async-done | bytes 214544
  (523 shorter events, 331.3 us)
Async XLA Ops:
  7.2 97.9 %all-gather.15.cloned.1.call-start = ((), (), s32[]{:S(2)}) async-start(), calls=%async_computation.21 | async-start | bytes 7299072 | tf_op jit(solution)/shard_map/all_gather | solution.py:204
  7.9 216.9 %all-gather.19.cloned.1.call-start = ((), (), s32[]{:S(2)}) async-start(), calls=%async_computation.23 | async-start | bytes 1081344 | tf_op jit(solution)/shard_map/all_gather | solution.py:205
  8.7 227.5 %all-gather.21.cloned.1.call-start = ((), (), s32[]{:S(2)}) async-start(), calls=%async_computation.24 | async-start | bytes 1081344 | tf_op jit(solution)/shard_map/all_gather | solution.py:208
  9.4 236.3 %all-gather.29.cloned.1.call-start = ((), (), s32[]{:S(2)}) async-start(), calls=%async_computation.46 | async-start | bytes 1966080 | tf_op jit(solution)/shard_map/all_gather | solution.py:28
  110.4 6.3 collective-permute-start
  127.5 153.8 %all-gather.17.cloned.1.call-start = ((), (), s32[]{:S(2)}) async-start(), calls=%async_computation.22 | async-start | bytes 3244032 | tf_op jit(solution)/shard_map/all_gather | solution.py:209
  128.1 216.8 %all-gather.23.cloned.1.call-start = ((), (), s32[]{:S(2)}) async-start(), calls=%async_computation.25 | async-start | bytes 4325376 | tf_op jit(solution)/shard_map/all_gather | solution.py:210
  128.7 279.8 %all-gather.25.cloned.1.call-start = ((), (), s32[]{:S(2)}) async-start(), calls=%async_computation.26 | async-start | bytes 4325376 | tf_op jit(solution)/shard_map/all_gather | solution.py:211
  129.4 342.5 %all-gather.27.cloned.1.call-start = ((), (), s32[]{:S(2)}) async-start(), calls=%async_computation.27 | async-start | bytes 4325376 | tf_op jit(solution)/shard_map/all_gather | solution.py:212
  130.2 393.6 %reduce-scatter.31.cloned.1.call-start = ((), (), s32[]{:S(2)}) async-start(), calls=%async_computation.29 | async-start | bytes 327680 | tf_op jit(solution)/shard_map/reduce_scatter | solution.py:404
  505.0 41.9 %reduce-scatter.29.cloned.1.call-start = ((), (), s32[]{:S(2)}) async-start(), calls=%async_computation.28 | async-start | bytes 327680 | tf_op jit(solution)/shard_map/reduce_scatter | solution.py:398
  514.4 97.0 %reduce-scatter.41.cloned.1.call-start = ((), (), s32[]{:S(2)}) async-start(), calls=%async_computation.34 | async-start | bytes 294912 | tf_op jit(solution)/shard_map/reduce_scatter | solution.py:465
  526.0 149.6 %reduce-scatter.37.cloned.1.call-start = ((), (), s32[]{:S(2)}) async-start(), calls=%async_computation.32 | async-start | bytes 294912 | tf_op jit(solution)/shard_map/reduce_scatter | solution.py:462
  549.1 192.4 %reduce-scatter.33.cloned.1.call-start = ((), (), s32[]{:S(2)}) async-start(), calls=%async_computation.30 | async-start | bytes 1179648 | tf_op jit(solution)/shard_map/reduce_scatter | solution.py:459
  554.7 253.1 %reduce-scatter.45.cloned.1.call-start = ((), (), s32[]{:S(2)}) async-start(), calls=%async_computation.36 | async-start | bytes 1179648 | tf_op jit(solution)/shard_map/reduce_scatter | solution.py:468
  557.3 271.1 %all-gather.31.cloned.1.call-start = ((), (), s32[]{:S(2)}) async-start(), calls=%async_computation.47 | async-start | bytes 1966080 | tf_op jit(solution)/shard_map/all_gather | solution.py:51
  577.9 328.4 %reduce-scatter.49.cloned.1.call-start = ((), (), s32[]{:S(2)}) async-start(), calls=%async_computation.38 | async-start | bytes 3538944 | tf_op jit(solution)/shard_map/reduce_scatter | solution.py:471
  582.0 414.7 %reduce-scatter.53.cloned.1.call-start = ((), (), s32[]{:S(2)}) async-start(), calls=%async_computation.40 | async-start | bytes 4718592 | tf_op jit(solution)/shard_map/reduce_scatter | solution.py:474
  586.7 501.7 %reduce-scatter.57.cloned.1.call-start = ((), (), s32[]{:S(2)}) async-start(), calls=%async_computation.42 | async-start | bytes 4718592 | tf_op jit(solution)/shard_map/reduce_scatter | solution.py:477
  591.2 588.7 %reduce-scatter.61.cloned.1.call-start = ((), (), s32[]{:S(2)}) async-start(), calls=%async_computation.44 | async-start | bytes 4718592 | tf_op jit(solution)/shard_map/reduce_scatter | solution.py:480
  595.9 605.5 %reduce-scatter.43.cloned.1.call-start = ((), (), s32[]{:S(2)}) async-start(), calls=%async_computation.35 | async-start | bytes 40960 | tf_op jit(solution)/shard_map/reduce_scatter | solution.py:509
  611.5 611.7 %reduce-scatter.39.cloned.1.call-start = ((), (), s32[]{:S(2)}) async-start(), calls=%async_computation.33 | async-start | bytes 40960 | tf_op jit(solution)/shard_map/reduce_scatter | solution.py:506
  675.6 588.3 %reduce-scatter.35.cloned.1.call-start = ((), (), s32[]{:S(2)}) async-start(), calls=%async_computation.31 | async-start | bytes 163840 | tf_op jit(solution)/shard_map/reduce_scatter | solution.py:503
  741.5 525.8 %reduce-scatter.47.cloned.1.call-start = ((), (), s32[]{:S(2)}) async-start(), calls=%async_computation.37 | async-start | bytes 163840 | tf_op jit(solution)/shard_map/reduce_scatter | solution.py:512
  807.8 592.6 %reduce-scatter.65.cloned.1.call-start = ((), (), s32[]{:S(2)}) async-start(), calls=%async_computation.48 | async-start | bytes 7962624
  864.1 3.2 collective-permute-start.1
  883.6 581.0 %reduce-scatter.69.cloned.1.call-start = ((), (), s32[]{:S(2)}) async-start(), calls=%async_computation.50 | async-start | bytes 516096
  885.4 601.6 %reduce-scatter.51.cloned.1.call-start = ((), (), s32[]{:S(2)}) async-start(), calls=%async_computation.39 | async-start | bytes 491520 | tf_op jit(solution)/shard_map/reduce_scatter | solution.py:515
  906.2 604.9 %reduce-scatter.55.cloned.1.call-start = ((), (), s32[]{:S(2)}) async-start(), calls=%async_computation.41 | async-start | bytes 655360 | tf_op jit(solution)/shard_map/reduce_scatter | solution.py:518
  996.8 538.5 %reduce-scatter.59.cloned.1.call-start = ((), (), s32[]{:S(2)}) async-start(), calls=%async_computation.43 | async-start | bytes 655360 | tf_op jit(solution)/shard_map/reduce_scatter | solution.py:521
  1088.4 471.2 %reduce-scatter.63.cloned.1.call-start = ((), (), s32[]{:S(2)}) async-start(), calls=%async_computation.45 | async-start | bytes 655360 | tf_op jit(solution)/shard_map/reduce_scatter | solution.py:524
  1179.9 406.0 %reduce-scatter.67.cloned.1.call-start = ((), (), s32[]{:S(2)}) async-start(), calls=%async_computation.49 | async-start | bytes 1105920
  (132 other events, 3095.7 us)
Sparse Core Ops, SparseCore 0:
  10.9 75.6 all-gather.14
  89.5 52.2 all-gather.18
  144.6 52.8 all-gather.20
  199.5 18.9 all-gather.28
  221.2 60.0 all-gather.16
  284.0 60.8 all-gather.22
  347.8 60.5 all-gather.24
  411.3 60.5 all-gather.26
  505.1 18.5 reduce-scatter.30
  526.8 20.0 reduce-scatter.28
  550.2 61.1 reduce-scatter.40
  615.2 60.3 reduce-scatter.36
  679.0 62.4 reduce-scatter.32
  745.1 62.5 reduce-scatter.44
  809.7 18.6 all-gather.30
  831.9 74.3 reduce-scatter.48
  909.7 87.0 reduce-scatter.52
  1000.7 87.6 reduce-scatter.56
  1092.0 87.7 reduce-scatter.60
  1182.3 19.0 reduce-scatter.42
  1203.8 19.3 reduce-scatter.38
  1225.7 19.5 reduce-scatter.34
  1247.8 19.5 reduce-scatter.46
  1271.3 129.0 reduce-scatter.64
  1403.7 60.8 reduce-scatter.68
  1467.1 19.7 reduce-scatter.50
  1489.4 21.6 reduce-scatter.54
  1513.6 21.6 reduce-scatter.58
  1537.9 21.6 reduce-scatter.62
  1562.0 23.8 reduce-scatter.66
where the time goes:
time: 1610 us; the launch traced here: 1600 us
  waiting for transfers between devices  1000 us (62%)
  blocking collectives  258 us (16%)
  matrix products  162 us (10%)
  other arithmetic  75.1 us (5%)
  local copies, waits for them, and re-layouts  68.2 us (4%)
  between operations  21.6 us (1%)
    unnamed x33, waiting for transfers between devices  179 us
    reduce_scatter x1, waiting for transfers between devices, body(): lax.psum_scatter(up_w_grad.astype(jnp.bfloat16), 'dp', scatter_dimension=...  91.6 us
    reduce_scatter x1, waiting for transfers between devices, body(): lax.psum_scatter(down_w_grad.astype(jnp.bfloat16), 'dp', scatter_dimensio...  91.4 us
    reduce_scatter x1, waiting for transfers between devices, body(): lax.psum_scatter(gate_w_grad.astype(jnp.bfloat16), 'dp', scatter_dimensio...  90.5 us
    unnamed x3, blocking collectives  83.4 us
    reduce_scatter x1, waiting for transfers between devices, body(): lax.psum_scatter(query_w_grad.astype(jnp.bfloat16), 'dp', scatter_dimensi...  63.7 us
    all_gather x1, waiting for transfers between devices, body(): lax.all_gather(up_proj, ('dp', 'seq'), axis=0, tiled=True)  58.6 us
    all_gather x1, waiting for transfers between devices, body(): lax.all_gather(down_proj, ('dp', 'seq'), axis=0, tiled=True)  58.6 us
  transfers between devices with their start and end apart: 32, of which 26 were waited for; matrix products, arithmetic and copies ran while one was open for 16% of the time, Pallas kernels for 0%

commit v1 on v0

v1 whole, which is shorter than its diff:
```python
import functools

import jax
import jax.numpy as jnp
from jax import lax
from jax.experimental import pallas as pl
from jax.experimental.pallas import tpu as pltpu
from jax.sharding import PartitionSpec as P

H = 24
P_SIZE = 64
N = 128
CONV = 4
NH = 8
KVH = 2
HD = 64
INNER = H * P_SIZE
CONV_W = INNER + 2 * N
Q_AT = INNER + CONV_W
K_AT = Q_AT + NH * HD
V_AT = K_AT + KVH * HD
RAW_AT = V_AT + KVH * HD
PACK = RAW_AT + H
BOTH = ("dp", "seq")
EPS = 1e-05
F32 = jnp.float32
BF = jnp.bfloat16
EXACT = lax.Precision.HIGHEST
VMEM = 48 * 1024 * 1024
SCALE = HD ** (-0.5)


def dot(a, b):
    return jnp.dot(a, b, preferred_element_type=F32)


def dot_ta(a, b):
    return lax.dot_general(a, b, (((0,), (0,)), ((), ())), preferred_element_type=F32)


def dot_tb(a, b):
    return lax.dot_general(a, b, (((1,), (1,)), ((), ())), preferred_element_type=F32)


def exact_dot(a, b):
    return jnp.dot(a, b, precision=EXACT, preferred_element_type=F32)


def gather_all(a):
    return lax.all_gather(a, BOTH, axis=0, tiled=True)


def scatter_all(a):
    return lax.psum_scatter(a.astype(BF), BOTH, scatter_dimension=0, tiled=True).astype(F32)


def column_of(block, at):
    lanes = lax.broadcasted_iota(jnp.int32, block.shape, 1)
    return jnp.sum(jnp.where(lanes == at, block, 0.0), axis=1, keepdims=True)


def decay_between(log_ref, log_row_ref, seg_col_ref, seg_row_ref, head):
    rows = log_ref.shape[0]
    at_row = lax.broadcasted_iota(jnp.int32, (rows, rows), 0)
    at_col = lax.broadcasted_iota(jnp.int32, (rows, rows), 1)
    allowed = (at_row >= at_col) & (seg_col_ref[...] == seg_row_ref[...])
    gap = column_of(log_ref[...], head) - log_row_ref[pl.ds(head, 1), :]
    return jnp.exp(jnp.where(allowed, gap, -10000.0))


def inner_forward_kernel(x_ref, g_ref, log_ref, log_row_ref, dt_row_ref, sc_ref, sr_ref, y_ref):
    pair = pl.program_id(0)
    x = x_ref[...]
    lanes = lax.broadcasted_iota(jnp.int32, x.shape, 1)
    parts = []
    for i in range(2):
        head = 2 * pair + i
        e = decay_between(log_ref, log_row_ref, sc_ref, sr_ref, head)
        mixing = (e * dt_row_ref[pl.ds(head, 1), :] * g_ref[...]).astype(BF)
        parts.append(dot(mixing, x))
    y_ref[...] = jnp.where(lanes < P_SIZE, parts[0], parts[1])


def inner_backward_kernel(
    x_ref, dy_ref, g_ref, log_ref, log_row_ref, dt_row_ref, sc_ref, sr_ref,
    dx_ref, dg_ref, row_ref, col_ref,
):
    pair = pl.program_id(0)

    @pl.when(pair == 0)
    def _():
        dg_ref[...] = jnp.zeros_like(dg_ref)
        row_ref[...] = jnp.zeros_like(row_ref)

    x = x_ref[...]
    dy = dy_ref[...]
    lanes = lax.broadcasted_iota(jnp.int32, x.shape, 1)
    row_lanes = lax.broadcasted_iota(jnp.int32, row_ref.shape, 1)
    parts = []
    for i in range(2):
        head = 2 * pair + i
        e = decay_between(log_ref, log_row_ref, sc_ref, sr_ref, head)
        dt = dt_row_ref[pl.ds(head, 1), :]
        g = g_ref[...]
        mine = (lanes < P_SIZE) if i == 0 else (lanes >= P_SIZE)
        dm = dot_tb(jnp.where(mine, dy, jnp.zeros_like(dy)), x)
        q = dm * e
        eg = e * g
        parts.append(dot_ta((eg * dt).astype(BF), dy))
        qd = q * dt
        dg_ref[...] += qd
        row_ref[...] += jnp.where(
            row_lanes == head, jnp.sum(qd * g, axis=1, keepdims=True), 0.0
        )
        col_ref[pl.ds(head, 1), :] = jnp.sum(q * g, axis=0, keepdims=True)
    dx_ref[...] = jnp.where(lanes < P_SIZE, parts[0], parts[1])


def whole(shape):
    return pl.BlockSpec(shape, lambda p: (0,) * len(shape))


def pair_block(rows):
    return pl.BlockSpec((rows, 2 * P_SIZE), lambda p: (0, p))


def params():
    return pltpu.CompilerParams(vmem_limit_bytes=VMEM)


def inner_forward(x, g, log_col, log_row, dt_row, seg_col, seg_row):
    t = x.shape[0]
    return pl.pallas_call(
        inner_forward_kernel,
        grid=(H // 2,),
        in_specs=[
            pair_block(t), whole((t, t)), whole((t, H)), whole((H, t)), whole((H, t)),
            whole((t, 1)), whole((1, t)),
        ],
        out_specs=pair_block(t),
        out_shape=jax.ShapeDtypeStruct((t, INNER), F32),
        compiler_params=params(),
        cost_estimate=pl.CostEstimate(
            flops=4 * H * t * t * P_SIZE, bytes_accessed=6 * t * INNER, transcendentals=H * t * t
        ),
    )(x, g, log_col, log_row, dt_row, seg_col, seg_row)


def inner_backward(x, dy, g, log_col, log_row, dt_row, seg_col, seg_row):
    t = x.shape[0]
    return pl.pallas_call(
        inner_backward_kernel,
        grid=(H // 2,),
        in_specs=[
            pair_block(t), pair_block(t), whole((t, t)), whole((t, H)), whole((H, t)),
            whole((H, t)), whole((t, 1)), whole((1, t)),
        ],
        out_specs=[pair_block(t), whole((t, t)), whole((t, H)), whole((H, t))],
        out_shape=[
            jax.ShapeDtypeStruct((t, INNER), F32),
            jax.ShapeDtypeStruct((t, t), F32),
            jax.ShapeDtypeStruct((t, H), F32),
            jax.ShapeDtypeStruct((H, t), F32),
        ],
        compiler_params=params(),
        cost_estimate=pl.CostEstimate(
            flops=8 * H * t * t * P_SIZE, bytes_accessed=8 * t * INNER, transcendentals=H * t * t
        ),
    )(x, dy, g, log_col, log_row, dt_row, seg_col, seg_row)


def head_scores(q, k_ref, allowed, lanes, i):
    mine = (lanes < HD) if i == 0 else (lanes >= HD)
    own = jnp.where(mine, q, jnp.zeros_like(q))
    return mine, own, jnp.where(allowed, dot_tb(own, k_ref[...]) * SCALE, -1e30)


def keys_allowed(first, sc_ref, sr_ref):
    shape = (sc_ref.shape[0], sr_ref.shape[1])
    at_row = lax.broadcasted_iota(jnp.int32, shape, 0) + first
    at_col = lax.broadcasted_iota(jnp.int32, shape, 1)
    return (at_row >= at_col) & (sc_ref[...] == sr_ref[...])


def attend_forward_kernel(q_ref, k_ref, v_ref, sc_ref, sr_ref, out_ref, lse_ref):
    first = lax.axis_index("seq") * q_ref.shape[0]
    allowed = keys_allowed(first, sc_ref, sr_ref)
    q = q_ref[...]
    lanes = lax.broadcasted_iota(jnp.int32, q.shape, 1)
    outs, totals = [], []
    for i in range(2):
        _, _, scores = head_scores(q, k_ref, allowed, lanes, i)
        top = jnp.max(scores, axis=1, keepdims=True)
        probs = jnp.exp(scores - top)
        total = jnp.sum(probs, axis=1, keepdims=True)
        outs.append(dot(probs.astype(BF), v_ref[...]) / total)
        totals.append(top + jnp.log(total))
    out_ref[...] = jnp.where(lanes < HD, outs[0], outs[1]).astype(BF)
    lse_ref[...] = jnp.where(lanes < HD, totals[0], totals[1])


def attend_backward_kernel(
    q_ref, k_ref, v_ref, dm_ref, lse_ref, sc_ref, sr_ref, dq_ref, dk_ref, dv_ref
):
    pair = pl.program_id(0)

    @pl.when(lax.rem(pair, NH // KVH // 2) == 0)
    def _():
        dk_ref[...] = jnp.zeros_like(dk_ref)
        dv_ref[...] = jnp.zeros_like(dv_ref)

    first = lax.axis_index("seq") * q_ref.shape[0]
    allowed = keys_allowed(first, sc_ref, sr_ref)
    q = q_ref[...]
    dmix = dm_ref[...]
    lanes = lax.broadcasted_iota(jnp.int32, q.shape, 1)
    dqs = []
    for i in range(2):
        mine, own, scores = head_scores(q, k_ref, allowed, lanes, i)
        probs = jnp.exp(scores - lse_ref[:, i * HD : i * HD + 1])
        down = jnp.where(mine, dmix, jnp.zeros_like(dmix))
        dp = dot_tb(down, v_ref[...])
        delta = jnp.sum(probs * dp, axis=1, keepdims=True)
        ds = (probs * (dp - delta)).astype(BF)
        dqs.append(dot(ds, k_ref[...]) * SCALE)
        dk_ref[...] += dot_ta(ds, own) * SCALE
        dv_ref[...] += dot_ta(probs.astype(BF), down)
    dq_ref[...] = jnp.where(lanes < HD, dqs[0], dqs[1]).astype(BF)


def kv_block(keys):
    per = NH // KVH // 2
    return pl.BlockSpec((keys, 2 * HD), lambda p: (0, p // per))


def attend_forward(q, k2, v2, seg_col, seg_row):
    t, keys = q.shape[0], k2.shape[0]
    return pl.pallas_call(
        attend_forward_kernel,
        grid=(NH // 2,),
        in_specs=[
            pair_block(t), kv_block(keys), kv_block(keys), whole((t, 1)), whole((1, keys)),
        ],
        out_specs=[pair_block(t), pair_block(t)],
        out_shape=[
            jax.ShapeDtypeStruct((t, NH * HD), BF),
            jax.ShapeDtypeStruct((t, NH * HD), F32),
        ],
        compiler_params=params(),
        cost_estimate=pl.CostEstimate(
            flops=8 * NH * t * keys * HD, bytes_accessed=2 << 20, transcendentals=NH * t * keys
        ),
    )(q, k2, v2, seg_col, seg_row)


def attend_backward(q, k2, v2, dmix, lse, seg_col, seg_row):
    t, keys = q.shape[0], k2.shape[0]
    return pl.pallas_call(
        attend_backward_kernel,
        grid=(NH // 2,),
        in_specs=[
            pair_block(t), kv_block(keys), kv_block(keys), pair_block(t), pair_block(t),
            whole((t, 1)), whole((1, keys)),
        ],
        out_specs=[pair_block(t), kv_block(keys), kv_block(keys)],
        out_shape=[
            jax.ShapeDtypeStruct((t, NH * HD), BF),
            jax.ShapeDtypeStruct((keys, 2 * KVH * HD), F32),
            jax.ShapeDtypeStruct((keys, 2 * KVH * HD), F32),
        ],
        compiler_params=params(),
        cost_estimate=pl.CostEstimate(
            flops=20 * NH * t * keys * HD, bytes_accessed=4 << 20, transcendentals=NH * t * keys
        ),
    )(q, k2, v2, dmix, lse, seg_col, seg_row)


def doubled(pair):
    a, b = pair[:, :HD], pair[:, HD:]
    return jnp.concatenate([a, a, b, b], axis=1)


def folded(wide):
    parts = [wide[:, i * HD : (i + 1) * HD] for i in range(2 * KVH)]
    return jnp.concatenate([parts[0] + parts[1], parts[2] + parts[3]], axis=1)


def carried_states(everything, coefs, size):
    total = 0.0
    for k in range(size):
        part = everything[k].reshape(H, P_SIZE, N).astype(F32)
        total = total + coefs[k][:, None, None] * part
    return total.reshape(INNER, N)


def norm_back(values, scale, gain, grad):
    weighted = gain * grad
    return scale * weighted - values * scale**3 * jnp.mean(
        values * weighted, axis=-1, keepdims=True
    )


def body(
    hidden_in,
    segments,
    cotangent,
    in_proj,
    query_proj,
    key_proj,
    value_proj,
    attn_proj,
    mixer_proj,
    gate_proj,
    up_proj,
    down_proj,
    conv_weight,
    conv_bias,
    norm_one,
    norm_two,
    mixer_norm,
    step_bias,
    decay_log,
    skip_gain,
):
    size, here = lax.axis_size("seq"), lax.axis_index("seq")
    owners = size * lax.axis_size("dp")
    t = hidden_in.shape[1]
    seq_length = segments.shape[1]
    own_conv, own_d, own_in = conv_weight.shape[0], norm_one.shape[0], mixer_norm.shape[0]
    width = own_d * owners

    small = jnp.concatenate(
        [conv_weight.T.reshape(-1), conv_bias, norm_one, norm_two, mixer_norm]
    )
    small = lax.all_gather(small, BOTH, axis=0)
    in_pack = gather_all(
        jnp.concatenate(
            [in_proj[:, :Q_AT], query_proj, key_proj, value_proj, in_proj[:, Q_AT:]], axis=1
        )
    )
    full_mixer = gather_all(mixer_proj)
    full_attn = gather_all(attn_proj)
    full_gu = gather_all(jnp.concatenate([gate_proj, up_proj], axis=1))
    full_down = gather_all(down_proj)

    cut = (CONV + 1) * own_conv
    conv_all = (
        small[:, :cut]
        .reshape(owners, CONV + 1, own_conv)
        .transpose(1, 0, 2)
        .reshape(CONV + 1, CONV_W)
        .astype(F32)
    )
    gains = (
        small[:, cut : cut + 2 * own_d]
        .reshape(owners, 2, own_d)
        .transpose(1, 0, 2)
        .reshape(2, width)
        .astype(F32)
    )
    gain_one, gain_two = gains[0], gains[1]
    mixer_gain = small[:, cut + 2 * own_d :].reshape(INNER).astype(F32)

    segs = segments[0]
    first = here * t
    padded_ids = jnp.concatenate([jnp.full((CONV - 1,), -1, jnp.int32), segs])
    ext_ids = lax.dynamic_slice_in_dim(padded_ids, first, t + CONV - 1, 0)
    ids = ext_ids[CONV - 1 :]
    before = ext_ids[CONV - 2]
    taps = [(ext_ids[j : j + t] == ids).astype(F32)[:, None] for j in range(CONV)]
    seg_col, seg_row, seg_all = ids[:, None], ids[None, :], segs[None, :]
    to_end = (ids == ids[-1]).astype(F32)[:, None]
    from_before = (ids == before).astype(F32)[:, None]
    across = (ids[-1] == before).astype(F32)
    lower = jnp.tril(jnp.ones((t, t), F32))
    spread = jnp.repeat(jnp.eye(H, dtype=F32), P_SIZE, axis=1)

    hidden = hidden_in[0].astype(F32)
    scale_one = lax.rsqrt(jnp.mean(hidden * hidden, axis=-1, keepdims=True) + EPS)
    normed = (hidden * scale_one * gain_one).astype(BF)
    proj = dot(normed, in_pack).astype(BF)
    query = proj[:, Q_AT:K_AT]
    conv_in = proj[:, INNER:Q_AT]
    pairs = [(i, i + 1) for i in range(size - 1)]
    rim = lax.ppermute(conv_in[t - CONV + 1 :], "seq", pairs)
    kv = lax.all_gather(proj[:, K_AT:RAW_AT], "seq", axis=0, tiled=True)
    gate_z = proj[:, :INNER].astype(F32)
    step_in = proj[:, RAW_AT:].astype(F32) + step_bias
    ext = jnp.concatenate([rim, conv_in], axis=0).astype(F32)

    running = conv_all[CONV]
    for j in range(CONV):
        running = running + conv_all[j] * ext[j : j + t] * taps[j]
    conv_sig = jax.nn.sigmoid(running)
    conv_out = running * conv_sig
    x = conv_out[:, :INNER]
    x_low = x.astype(BF)
    write = conv_out[:, INNER : INNER + N].astype(BF)
    read = conv_out[:, INNER + N :].astype(BF)
    dt = jax.nn.softplus(step_in)
    rate = -jnp.exp(decay_log)
    log_decay = exact_dot(lower, dt * rate)
    log_row, dt_row = log_decay.T, dt.T
    end_bare = jnp.exp(log_decay[-1:] - log_decay) * to_end
    end_weight = end_bare * dt
    from_state = jnp.exp(log_decay) * from_before
    wide = exact_dot(jnp.concatenate([end_weight, from_state], axis=0), spread)
    end_wide, from_wide = wide[:t], wide[t:]
    skip_wide = jnp.repeat(skip_gain, P_SIZE)
    xw = (x * end_wide).astype(BF)
    state_local = dot_ta(xw, write)
    block_decay = jnp.exp(log_decay[-1]) * across
    decay_rows = jnp.pad(block_decay[None, :], ((0, 15), (0, N - H)))
    states = lax.all_gather(
        jnp.concatenate([state_local, decay_rows], axis=0).astype(BF), "seq", axis=0
    )
    decays = states[:, INNER, :H].astype(F32)
    ones = jnp.ones((H,), F32)
    fore, back = [None] * size, [None] * size
    run = ones
    for k in range(size - 1, -1, -1):
        inside = k < here
        fore[k] = jnp.where(inside, run, 0.0)
        run = jnp.where(inside, run * decays[k], run)
    run = ones
    for k in range(size):
        inside = k > here
        back[k] = jnp.where(inside, run, 0.0)
        run = jnp.where(inside, run * decays[k], run)
    state_f = carried_states(states[:, :INNER], fore, size)
    state_in = state_f.astype(BF)

    gram = dot_tb(read, write)
    inner = inner_forward(x_low, gram, log_decay, log_row, dt_row, seg_col, seg_row)
    from_read = dot_tb(read, state_in)
    ssm_out = inner + from_wide * from_read + skip_wide * x
    sig_z = jax.nn.sigmoid(gate_z)
    silu_z = gate_z * sig_z
    gated = ssm_out * silu_z
    scale_mix = lax.rsqrt(jnp.mean(gated * gated, axis=-1, keepdims=True) + EPS)
    mixed = (gated * scale_mix * mixer_gain).astype(BF)

    k2, v2 = doubled(kv[:, : KVH * HD]), doubled(kv[:, KVH * HD :])
    attn_mix, lse = attend_forward(query, k2, v2, seg_col, seg_all)
    resid = hidden + dot(mixed, full_mixer) + dot(attn_mix, full_attn)
    scale_two = lax.rsqrt(jnp.mean(resid * resid, axis=-1, keepdims=True) + EPS)
    normed_two = (resid * scale_two * gain_two).astype(BF)
    ff = full_gu.shape[1] // 2
    gate_up = dot(normed_two, full_gu)
    gate_val, up_val = gate_up[:, :ff], gate_up[:, ff:]
    sig_g = jax.nn.sigmoid(gate_val)
    activated = (gate_val * sig_g * up_val).astype(BF)
    layer_out = (resid + dot(activated, full_down)).astype(BF)

    cot = cotangent[0]
    down_w = scatter_all(dot_ta(activated, cot))
    act_grad = dot_tb(cot, full_down)
    gate_grad = act_grad * up_val * sig_g * (1.0 + gate_val * (1.0 - sig_g))
    up_grad = act_grad * gate_val * sig_g
    gu_grad = jnp.concatenate([gate_grad.astype(BF), up_grad.astype(BF)], axis=1)
    gu_w = scatter_all(dot_ta(normed_two, gu_grad))
    normed_two_grad = dot_tb(gu_grad, full_gu)
    two_grad = jnp.sum(resid * scale_two * normed_two_grad, axis=0)
    resid_grad = cot.astype(F32) + norm_back(resid, scale_two, gain_two, normed_two_grad)
    resid_low = resid_grad.astype(BF)
    mixed_grad = dot_tb(resid_low, full_mixer)
    mix_grad = dot_tb(resid_low, full_attn).astype(BF)

    gain_grad = jnp.sum(gated * scale_mix * mixed_grad, axis=0)
    gated_grad = norm_back(gated, scale_mix, mixer_gain, mixed_grad)
    out_grad = gated_grad * silu_z
    gate_z_grad = gated_grad * ssm_out * sig_z * (1.0 + gate_z * (1.0 - sig_z))
    out_low = out_grad.astype(BF)
    out_from = (out_grad * from_wide).astype(BF)
    state_grad = dot_ta(out_from, read).astype(BF)
    state_grads = lax.all_gather(state_grad, "seq", axis=0)

    query_grad, dk2, dv2 = attend_backward(query, k2, v2, mix_grad, lse, seg_col, seg_all)
    kv_grad = lax.psum_scatter(
        jnp.concatenate([folded(dk2), folded(dv2)], axis=1).astype(BF),
        "seq",
        scatter_dimension=0,
        tiled=True,
    )
    mixer_w = scatter_all(dot_ta(mixed, resid_low))
    attn_w = scatter_all(dot_ta(attn_mix, resid_low))

    inner_x, gram_grad, row_sum, col_sum = inner_backward(
        x_low, out_low, gram, log_decay, log_row, dt_row, seg_col, seg_row
    )
    gram_low = gram_grad.astype(BF)
    skip_grad = jnp.sum(jnp.sum(out_grad * x, axis=0).reshape(H, P_SIZE), axis=1)
    later_f = carried_states(state_grads, back, size)
    later = later_f.astype(BF)
    decay_grad = jnp.sum((later_f * state_f).reshape(H, P_SIZE * N), axis=1)
    from_write = dot_tb(write, later)
    x_grad = inner_x + skip_wide * out_grad + end_wide * from_write
    write_grad = dot_ta(gram_low, read) + dot(xw, later)
    read_grad = dot(gram_low, write) + dot(out_from, state_in)
    sums = exact_dot(
        jnp.concatenate([out_grad * from_read, x * from_write], axis=0), spread.T
    )
    from_grad, end_grad = sums[:t] * from_state, sums[t:]
    end_part = end_weight * end_grad
    dt_part = col_sum.T
    log_grad = row_sum - dt * dt_part + from_grad - end_part
    last = (jnp.arange(t) == t - 1).astype(F32)[:, None]
    log_grad = log_grad + last * (jnp.sum(end_part, axis=0) + block_decay * decay_grad)
    rate_grad = exact_dot(lower.T, log_grad)
    dt_grad = dt_part + end_bare * end_grad + rate_grad * rate
    decay_log_grad = jnp.sum(rate_grad * dt * rate, axis=0)
    raw_grad = dt_grad * jax.nn.sigmoid(step_in)
    step_bias_grad = jnp.sum(raw_grad, axis=0)

    conv_grad = jnp.concatenate([x_grad, write_grad, read_grad], axis=1)
    sum_grad = conv_grad * conv_sig * (1.0 + running * (1.0 - conv_sig))
    conv_b_grad = jnp.sum(sum_grad, axis=0)
    conv_w_grads = []
    ext_grad = 0.0
    for j in range(CONV):
        counted = sum_grad * taps[j]
        conv_w_grads.append(jnp.sum(counted * ext[j : j + t], axis=0))
        ext_grad = ext_grad + jnp.pad(counted * conv_all[j], ((j, CONV - 1 - j), (0, 0)))
    rim_grad = lax.ppermute(ext_grad[: CONV - 1], "seq", [(b, a) for a, b in pairs])
    conv_in_grad = ext_grad[CONV - 1 :] + jnp.pad(rim_grad, ((t - CONV + 1, 0), (0, 0)))
    pack_grad = jnp.concatenate(
        [
            gate_z_grad.astype(BF),
            conv_in_grad.astype(BF),
            query_grad,
            kv_grad,
            raw_grad.astype(BF),
        ],
        axis=1,
    )
    pack_w = scatter_all(dot_ta(normed, pack_grad))
    normed_grad = dot_tb(pack_grad, in_pack)
    one_grad = jnp.sum(hidden * scale_one * normed_grad, axis=0)
    input_grad = resid_grad + norm_back(hidden, scale_one, gain_one, normed_grad)

    conv_grads = jnp.stack(conv_w_grads + [conv_b_grad])
    norm_grads = jnp.stack([one_grad, two_grad])
    small_grad = jnp.concatenate(
        [
            conv_grads.reshape(CONV + 1, owners, own_conv).transpose(1, 0, 2).reshape(owners, cut),
            norm_grads.reshape(2, owners, own_d).transpose(1, 0, 2).reshape(owners, 2 * own_d),
            gain_grad.reshape(owners, own_in),
        ],
        axis=1,
    )
    small_own = scatter_all(small_grad)[0]
    head_sums = lax.psum(jnp.stack([step_bias_grad, decay_log_grad, skip_grad]), BOTH)
    taps_cut = CONV * own_conv
    return (
        layer_out[None],
        input_grad[None],
        jnp.concatenate([pack_w[:, :Q_AT], pack_w[:, RAW_AT:]], axis=1),
        pack_w[:, Q_AT:K_AT],
        pack_w[:, K_AT:V_AT],
        pack_w[:, V_AT:RAW_AT],
        attn_w,
        mixer_w,
        gu_w[:, :ff],
        gu_w[:, ff:],
        down_w,
        small_own[:taps_cut].reshape(CONV, own_conv).T,
        small_own[taps_cut:cut],
        small_own[cut : cut + own_d],
        small_own[cut + own_d : cut + 2 * own_d],
        small_own[cut + 2 * own_d :],
        head_sums[0],
        head_sums[1],
        head_sums[2],
    )


def solution(mesh):
    placed = (
        P("dp", "seq", None),
        P("dp", None),
        P("dp", "seq", None),
        P(("dp", "seq"), None),
        P(("dp", "seq"), None),
        P(("dp", "seq"), None),
        P(("dp", "seq"), None),
        P(("dp", "seq"), None),
        P(("dp", "seq"), None),
        P(("dp", "seq"), None),
        P(("dp", "seq"), None),
        P(("dp", "seq"), None),
        P(("dp", "seq"), None),
        P(("dp", "seq")),
        P(("dp", "seq")),
        P(("dp", "seq")),
        P(("dp", "seq")),
        P(),
        P(),
        P(),
    )
    return jax.shard_map(
        body,
        mesh=mesh,
        in_specs=placed,
        out_specs=(
            P("dp", "seq", None),
            P("dp", "seq", None),
            P(("dp", "seq"), None),
            P(("dp", "seq"), None),
            P(("dp", "seq"), None),
            P(("dp", "seq"), None),
            P(("dp", "seq"), None),
            P(("dp", "seq"), None),
            P(("dp", "seq"), None),
            P(("dp", "seq"), None),
            P(("dp", "seq"), None),
            P(("dp", "seq"), None),
            P(("dp", "seq")),
            P(("dp", "seq")),
            P(("dp", "seq")),
            P(("dp", "seq")),
            P(),
            P(),
            P(),
        ),
        check_vma=False,
    )
```

time: 1610 us -> 1150 us (0.71)
  waiting for transfers between devices: 1000 us -> 762 us
  blocking collectives: 258 us -> 132 us
  matrix products: 162 us -> 99.3 us
  Pallas kernels: 0 us -> 29.8 us
  other arithmetic: 75.1 us -> 49.1 us
  local copies, waits for them, and re-layouts: 68.2 us -> 47.2 us
    unnamed x33 -> x13, waiting for transfers between devices: 179 us -> 1.89 us
    all_gather x6 -> x1, blocking collectives: 135 us -> 10.9 us  [body(): kv = lax.all_gather(proj[:, K_AT:RAW_AT], 'seq', axis=0, tiled=True)]
    reduce_scatter x18 -> x6, waiting for transfers between devices: 617 us -> 509 us  [the longest x5 509 us: scatter_all(): lax.psum_scatter(a.astype(BF), BOTH, scatter_dimension=0, tiled=True)]
    dot_general x45 -> x28, matrix products: 162 us -> 99.3 us  [the longest x8 38 us: dot_ta(): lax.dot_general(a, b, (((0,), (0,)), ((), ())), preferred_element_type=F32)]
    all_gather x9 -> x7, waiting for transfers between devices: 209 us -> 252 us  [the longest x5 252 us: gather_all(): return lax.all_gather(a, BOTH, axis=0, tiled=True)]
    pallas_call x0 -> x4, Pallas kernels: none -> 29.8 us  [the longest x1 9.93 us: attend_backward(): pl.pallas_call(attend_backward_kernel, grid=(NH // 2,), in_specs=[pair_bl...]
    unnamed x281 -> x276, local copies, waits for them, and re-layouts: 37.3 us -> 21 us
    unnamed x3 -> x2, blocking collectives: 83.4 us -> 83.8 us
  transfers between devices with their start and end apart: 32 -> 15, of which waited for: 26 -> 10; matrix products, arithmetic and copies ran while one was open for 16% -> 12% of each run, Pallas kernels for 0% -> 3%
where the time goes in v1:
time: 1150 us; the launch traced here: 1140 us
  waiting for transfers between devices  762 us (66%)
  blocking collectives  132 us (11%)
  matrix products  99.3 us (9%)
  other arithmetic  49.1 us (4%)
  local copies, waits for them, and re-layouts  47.2 us (4%)
  Pallas kernels  29.8 us (3%)
  between operations  17.4 us (2%)
    reduce_scatter x5, waiting for transfers between devices, scatter_all(): lax.psum_scatter(a.astype(BF), BOTH, scatter_dimension=0, tiled=True)  509 us
    all_gather x5, waiting for transfers between devices, gather_all(): return lax.all_gather(a, BOTH, axis=0, tiled=True)  252 us
    unnamed x2, blocking collectives  83.8 us
    dot_general x8, matrix products, dot_ta(): lax.dot_general(a, b, (((0,), (0,)), ((), ())), preferred_element_type=F32)  38 us
    psum x1, blocking collectives, body(): lax.psum(jnp.stack([step_bias_grad, decay_log_grad, skip_grad]), BOTH)  37.1 us
    dot_general x8, matrix products, dot(): return jnp.dot(a, b, preferred_element_type=F32)  29.3 us
    dot_general x8, matrix products, dot_tb(): lax.dot_general(a, b, (((1,), (1,)), ((), ())), preferred_element_type=F32)  24.9 us
  transfers between devices with their start and end apart: 15, of which 10 were waited for; matrix products, arithmetic and copies ran while one was open for 12% of the time, Pallas kernels for 3%

profile of v1, /device:TPU:0, one launch (start us, length us, event | category | flops | bytes accessed | tf_op | source)
XLA Modules:
  0.0 1141.3 jit_solution(14202610543957409583)
XLA Ops:
  18.4 42.5 %all-reduce.7 = bf16[12544]{0:T(1024)(128)(2,1)S(1)} all-reduce(bf16[12544]{0:T(1024)(128)(2,1)S(1)} %dynamic-update-slice), channel_id=2, replica_groups=mesh['dp'=8,'seq'=4] {'dp','seq'}, use_global_device_ids=true, to_apply=%add.7 | all-reduce | flops 12544 | bytes 50176
  64.6 28.7 %all-gather.10.cloned.1.call-done = bf16[1024,4120]{1,0:T(8,128)(2,1)} async-done(((bf16[32,4120]{1,0:T(8,128)(2,1)}), bf16[1024,4120]{1,0:T(8,128)(2,1)}) %all-gather.10.cloned.1.call-update) | async-done | bytes 8437776 | tf_op jit(solution)/shard_map/all_gather | solution.py:50
  93.4 6.0 convolution_convert_fusion.2
  115.6 10.9 all_gather.39
  127.5 6.2 shard_map.340
  137.1 5.5 shard_map.339
  149.3 4.7 multiply_reduce_fusion.7
  154.1 38.9 %all-gather.14.cloned.1.call-done = bf16[1536,1024]{1,0:T(8,128)(2,1)} async-done(((bf16[48,1024]{1,0:T(8,128)(2,1)}), bf16[1536,1024]{1,0:T(8,128)(2,1)}) %all-gather.14.cloned.1.call-update) | async-done | bytes 3145744 | tf_op jit(solution)/shard_map/all_gather | solution.py:50
  193.0 4.4 convert_add_fusion
  197.3 51.0 %all-gather.16.cloned.1.call-done = bf16[512,1024]{1,0:T(8,128)(2,1)} async-done(((bf16[16,1024]{1,0:T(8,128)(2,1)}), bf16[512,1024]{1,0:T(8,128)(2,1)}) %all-gather.16.cloned.1.call-update) | async-done | bytes 1048592 | tf_op jit(solution)/shard_map/all_gather | solution.py:50
  250.4 77.6 %all-gather.18.cloned.1.call-done = bf16[1024,4096]{1,0:T(8,128)(2,1)} async-done(((bf16[32,4096]{1,0:T(8,128)(2,1)}), bf16[1024,4096]{1,0:T(8,128)(2,1)}) %all-gather.18.cloned.1.call-update) | async-done | bytes 8388624 | tf_op jit(solution)/shard_map/all_gather | solution.py:50
  328.1 7.8 fusion.115
  335.9 55.5 %all-gather.20.cloned.1.call-done = bf16[2048,1024]{1,0:T(8,128)(2,1)} async-done(((bf16[64,1024]{1,0:T(8,128)(2,1)}), bf16[2048,1024]{1,0:T(8,128)(2,1)}) %all-gather.20.cloned.1.call-update) | async-done | bytes 4194320 | tf_op jit(solution)/shard_map/all_gather | solution.py:50
  391.5 6.6 multiply_convert_fusion.1
  410.7 11.4 %convolution_convert_fusion.5 = bf16[1536,128]{1,0:T(8,128)(2,1)} fusion(bf16[256,1536]{1,0:T(8,128)(2,1)S(1)} %get-tuple-element.83, bf16[256,1792]{1,0:T(8,128)(2,1)} %copy-done.56), kind=kOutput, calls=%fused_computation.9 | convolution fusion | flops 100859904 | bytes 1245184 | tf_op jit(solution)/shard_map/dot_general | solution.py:38
  424.2 9.9 shard_map.342
  438.8 3.9 convolution_convert_fusion.3
  444.0 3.3 convolution_convert_fusion.4
  453.5 8.1 shard_map.341
  469.5 4.0 fusion.51
  473.6 4.5 fusion.37
  501.8 7.6 convolution_convert_fusion
  511.0 7.1 convolution_convert_fusion.1
  519.3 4.2 fusion.18
  523.6 79.0 %reduce-scatter.11.cloned.1.call-done = bf16[16,1024]{1,0:T(8,128)(2,1)} async-done(((bf16[512,1024]{1,0:T(8,128)(2,1)}), bf16[16,1024]{1,0:T(8,128)(2,1)}) %reduce-scatter.11.cloned.1.call-update) | async-done | bytes 32784 | tf_op jit(solution)/shard_map/reduce_scatter | solution.py:54
  604.7 37.1 %psum.7 = f32[3,24]{1,0:T(4,128)S(1)} all-reduce(f32[3,24]{1,0:T(4,128)S(1)} %pad_maximum_fusion.10), channel_id=1, replica_groups=mesh['dp'=8,'seq'=4] {'dp','seq'}, use_global_device_ids=true, to_apply=%region_28.29 | all-reduce | flops 72 | bytes 576 | tf_op jit(solution)/shard_map/psum | solution.py:552
  642.3 6.9 fusion.20
  649.5 41.3 %all-reduce.8 = bf16[32,392]{1,0:T(8,128)(2,1)S(1)} all-reduce(bf16[32,392]{1,0:T(8,128)(2,1)S(1)} %pad_maximum_fusion.9), channel_id=10, replica_groups=mesh['dp'=8,'seq'=4] {'dp','seq'}, use_global_device_ids=true, to_apply=%region_23.24.clone | all-reduce | flops 12544 | bytes 50176
  694.5 11.4 reduce-scatter.13.cloned.1.call-done
  707.5 141.1 %reduce-scatter.17.cloned.1.call-done = bf16[64,1024]{1,0:T(8,128)(2,1)} async-done(((bf16[2048,1024]{1,0:T(8,128)(2,1)}), bf16[64,1024]{1,0:T(8,128)(2,1)}) %reduce-scatter.17.cloned.1.call-update) | async-done | bytes 131088 | tf_op jit(solution)/shard_map/reduce_scatter | solution.py:54
  850.2 131.8 %reduce-scatter.9.cloned.1.call-done = bf16[32,4120]{1,0:T(8,128)(2,1)} async-done(((bf16[1024,4120]{1,0:T(8,128)(2,1)}), bf16[32,4120]{1,0:T(8,128)(2,1)}) %reduce-scatter.9.cloned.1.call-update) | async-done | bytes 263696 | tf_op jit(solution)/shard_map/reduce_scatter | solution.py:54
  987.2 145.3 %reduce-scatter.15.cloned.1.call-done = bf16[32,4096]{1,0:T(8,128)(2,1)} async-done(((bf16[1024,4096]{1,0:T(8,128)(2,1)}), bf16[32,4096]{1,0:T(8,128)(2,1)}) %reduce-scatter.15.cloned.1.call-update) | async-done | bytes 262160 | tf_op jit(solution)/shard_map/reduce_scatter | solution.py:54
  (454 shorter events, 119.4 us)
Async XLA Ops:
  7.2 55.3 %copy-start.44 = (bf16[1,256,1024]{2,1,0:T(8,128)(2,1)S(1)}, bf16[1,256,1024]{2,1,0:T(8,128)(2,1)}, u32[]{:S(2)}) copy-start(bf16[1,256,1024]{2,1,0:T(8,128)(2,1)} %param.20) | copy-start | bytes 1572868
  7.2 55.5 %copy-start.128 = (f32[24]{0:T(128)S(1)}, f32[24]{0:T(128)}, u32[]{:S(2)}) copy-start(f32[24]{0:T(128)} %param.38) | copy-start | bytes 292
  7.2 86.1 %all-gather.10.cloned.1.call-start = ((), (), s32[]{:S(2)}) async-start(), calls=%async_computation.6 | async-start | bytes 8921088 | tf_op jit(solution)/shard_map/all_gather | solution.py:50
  11.9 130.8 %all-gather.12.cloned.1.call-start = ((), (), s32[]{:S(2)}) async-start(), calls=%async_computation.7 | async-start | bytes 1986560 | tf_op jit(solution)/shard_map/all_gather | solution.py:414
  62.1 43.9 %copy-start.90 = (f32[1792]{0:T(1024)}, f32[1792]{0:T(1024)S(1)}, u32[]{:S(2)}) copy-start(f32[1792]{0:T(1024)S(1)} %mul.674) | copy-start | bytes 21508
  62.2 43.8 %copy-start.92 = (f32[1792]{0:T(1024)}, f32[1792]{0:T(1024)S(1)}, u32[]{:S(2)}) copy-start(f32[1792]{0:T(1024)S(1)} %mul.686) | copy-start | bytes 21508
  62.3 43.7 %copy-start.94 = (f32[1792]{0:T(1024)}, f32[1792]{0:T(1024)S(1)}, u32[]{:S(2)}) copy-start(f32[1792]{0:T(1024)S(1)} %mul.691) | copy-start | bytes 21508
  62.4 43.6 %copy-start.96 = (f32[1792]{0:T(1024)}, f32[1792]{0:T(1024)S(1)}, u32[]{:S(2)}) copy-start(f32[1792]{0:T(1024)S(1)} %mul.696) | copy-start | bytes 21508
  64.6 41.4 %copy-start.108 = (f32[256]{0:T(256)}, f32[256]{0:T(256)S(1)}, u32[]{:S(2)}) copy-start(f32[256]{0:T(256)S(1)} %get-tuple-element.117) | copy-start | bytes 3076
  64.6 41.4 %copy-start.110 = (f32[256]{0:T(256)}, f32[256]{0:T(256)S(1)}, u32[]{:S(2)}) copy-start(f32[256]{0:T(256)S(1)} %get-tuple-element.118) | copy-start | bytes 3076
  100.8 5.0 collective-permute-start
  112.1 80.9 %all-gather.14.cloned.1.call-start = ((), (), s32[]{:S(2)}) async-start(), calls=%async_computation.8 | async-start | bytes 3244032 | tf_op jit(solution)/shard_map/all_gather | solution.py:50
  112.8 135.5 %all-gather.16.cloned.1.call-start = ((), (), s32[]{:S(2)}) async-start(), calls=%async_computation.9 | async-start | bytes 1081344 | tf_op jit(solution)/shard_map/all_gather | solution.py:50
  113.4 214.7 %all-gather.18.cloned.1.call-start = ((), (), s32[]{:S(2)}) async-start(), calls=%async_computation.10 | async-start | bytes 8650752 | tf_op jit(solution)/shard_map/all_gather | solution.py:50
  114.2 277.3 %all-gather.20.cloned.1.call-start = ((), (), s32[]{:S(2)}) async-start(), calls=%async_computation.11 | async-start | bytes 4325376 | tf_op jit(solution)/shard_map/all_gather | solution.py:50
  114.8 358.8 %all-gather.22.cloned.1.call-start = ((), (), s32[]{:S(2)}) async-start(), calls=%async_computation.18 | async-start | bytes 1966080 | tf_op jit(solution)/shard_map/all_gather | solution.py:476
  115.5 285.7 %copy-start.70 = (f32[1024]{0:T(1024)}, f32[1024]{0:T(1024)S(1)}, u32[]{:S(2)}) copy-start(f32[1024]{0:T(1024)S(1)} %mul.742) | copy-start | bytes 12292
  149.3 43.7 %copy-start.45 = (bf16[1,256,1024]{2,1,0:T(8,128)(2,1)S(1)}, bf16[1,256,1024]{2,1,0:T(8,128)(2,1)}, u32[]{:S(2)}) copy-start(bf16[1,256,1024]{2,1,0:T(8,128)(2,1)} %param.20) | copy-start | bytes 1572868
  154.1 250.8 %copy-start.77 = (f32[256]{0:T(256)}, f32[256]{0:T(256)S(1)}, u32[]{:S(2)}) copy-start(f32[256]{0:T(256)S(1)} %get-tuple-element.124) | copy-start | bytes 3076
  154.1 250.8 %copy-start.112 = (f32[256]{0:T(256)}, f32[256]{0:T(256)S(1)}, u32[]{:S(2)}) copy-start(f32[256]{0:T(256)S(1)} %get-tuple-element.123) | copy-start | bytes 3076
  250.4 150.8 %copy-start.34 = (f32[256,1024]{1,0:T(8,128)}, f32[256,1024]{1,0:T(8,128)S(1)}, u32[]{:S(2)}) copy-start(f32[256,1024]{1,0:T(8,128)S(1)} %get-tuple-element.128) | copy-start | bytes 3145732
  250.4 150.8 %copy-start.100 = (f32[256]{0:T(256)}, f32[256]{0:T(256)S(1)}, u32[]{:S(2)}) copy-start(f32[256]{0:T(256)S(1)} %get-tuple-element.126) | copy-start | bytes 3076
  328.1 63.4 %copy-start.57 = (bf16[1,256,1024]{2,1,0:T(8,128)(2,1)S(1)}, bf16[1,256,1024]{2,1,0:T(8,128)(2,1)}, u32[]{:S(2)}) copy-start(bf16[1,256,1024]{2,1,0:T(8,128)(2,1)} %param.22) | copy-start | bytes 1572868
  422.1 77.5 %reduce-scatter.7.cloned.1.call-start = ((), (), s32[]{:S(2)}) async-start(), calls=%async_computation.12 | async-start | bytes 655360 | tf_op jit(solution)/shard_map/reduce_scatter | solution.py:479
  436.0 166.6 %reduce-scatter.11.cloned.1.call-start = ((), (), s32[]{:S(2)}) async-start(), calls=%async_computation.14 | async-start | bytes 1081344 | tf_op jit(solution)/shard_map/reduce_scatter | solution.py:54
  438.7 267.2 %reduce-scatter.13.cloned.1.call-start = ((), (), s32[]{:S(2)}) async-start(), calls=%async_computation.15 | async-start | bytes 3244032 | tf_op jit(solution)/shard_map/reduce_scatter | solution.py:54
  442.7 405.9 %reduce-scatter.17.cloned.1.call-start = ((), (), s32[]{:S(2)}) async-start(), calls=%async_computation.17 | async-start | bytes 4325376 | tf_op jit(solution)/shard_map/reduce_scatter | solution.py:54
  447.3 534.8 %reduce-scatter.9.cloned.1.call-start = ((), (), s32[]{:S(2)}) async-start(), calls=%async_computation.13 | async-start | bytes 8921088 | tf_op jit(solution)/shard_map/reduce_scatter | solution.py:54
  490.7 7.0 collective-permute-start.1
  509.5 623.0 %reduce-scatter.15.cloned.1.call-start = ((), (), s32[]{:S(2)}) async-start(), calls=%async_computation.16 | async-start | bytes 8650752 | tf_op jit(solution)/shard_map/reduce_scatter | solution.py:54
  642.3 50.9 %copy-start.52 = (f32[256,1024]{1,0:T(8,128)S(1)}, f32[256,1024]{1,0:T(8,128)}, u32[]{:S(2)}) copy-start(f32[256,1024]{1,0:T(8,128)} %get-tuple-element.63) | copy-start | bytes 3145732
  642.3 50.9 %copy-start.115 = (f32[256]{0:T(256)S(1)}, f32[256]{0:T(256)}, u32[]{:S(2)}) copy-start(f32[256]{0:T(256)} %get-tuple-element.121) | copy-start | bytes 3076
  (115 other events, 709.4 us)
Sparse Core Ops, SparseCore 0:
  12.0 81.3 all-gather.9
  112.2 20.6 all-gather.11
  135.8 57.0 all-gather.13
  195.7 52.6 all-gather.15
  251.6 76.4 all-gather.17
  330.8 60.6 all-gather.19
  422.3 18.1 all-gather.21
  443.6 21.6 reduce-scatter.6
  467.6 134.8 reduce-scatter.10
  607.8 98.0 reduce-scatter.12
  708.2 140.3 reduce-scatter.16
  854.4 127.6 reduce-scatter.8
  984.3 148.1 reduce-scatter.14

commit v2 on v1

--- a/solution.py
+++ b/solution.py
@@ -332,16 +332,23 @@
     small = jnp.concatenate(
         [conv_weight.T.reshape(-1), conv_bias, norm_one, norm_two, mixer_norm]
     )
-    small = lax.all_gather(small, BOTH, axis=0)
+    n_small = small.shape[0]
+    extra = -(-n_small // own_d)
+    small = jnp.pad(small, (0, extra * own_d - n_small)).reshape(own_d, extra)
     in_pack = gather_all(
         jnp.concatenate(
-            [in_proj[:, :Q_AT], query_proj, key_proj, value_proj, in_proj[:, Q_AT:]], axis=1
+            [in_proj[:, :Q_AT], query_proj, key_proj, value_proj, in_proj[:, Q_AT:], small], axis=1
         )
     )
-    full_mixer = gather_all(mixer_proj)
-    full_attn = gather_all(attn_proj)
+    small = in_pack[:, PACK:].reshape(owners, own_d * extra)
+    own_rows = [down_proj.shape[0], mixer_proj.shape[0], attn_proj.shape[0]]
+    rows_at = [0, own_rows[0], own_rows[0] + own_rows[1], sum(own_rows)]
+    tall = gather_all(jnp.concatenate([down_proj, mixer_proj, attn_proj], axis=0))
+    tall = tall.reshape(owners, rows_at[3], -1)
+    full_down, full_mixer, full_attn = [
+        tall[:, rows_at[i] : rows_at[i + 1]].reshape(owners * own_rows[i], -1) for i in range(3)
+    ]
     full_gu = gather_all(jnp.concatenate([gate_proj, up_proj], axis=1))
-    full_down = gather_all(down_proj)
 
     cut = (CONV + 1) * own_conv
     conv_all = (
@@ -359,7 +366,7 @@
         .astype(F32)
     )
     gain_one, gain_two = gains[0], gains[1]
-    mixer_gain = small[:, cut + 2 * own_d :].reshape(INNER).astype(F32)
+    mixer_gain = small[:, cut + 2 * own_d : n_small].reshape(INNER).astype(F32)
 
     segs = segments[0]
     first = here * t
@@ -385,7 +392,7 @@
     rim = lax.ppermute(conv_in[t - CONV + 1 :], "seq", pairs)
     kv = lax.all_gather(proj[:, K_AT:RAW_AT], "seq", axis=0, tiled=True)
     gate_z = proj[:, :INNER].astype(F32)
-    step_in = proj[:, RAW_AT:].astype(F32) + step_bias
+    step_in = proj[:, RAW_AT:PACK].astype(F32) + step_bias
     ext = jnp.concatenate([rim, conv_in], axis=0).astype(F32)
 
     running = conv_all[CONV]
@@ -453,12 +460,12 @@
     layer_out = (resid + dot(activated, full_down)).astype(BF)
 
     cot = cotangent[0]
-    down_w = scatter_all(dot_ta(activated, cot))
+    down_w = dot_ta(activated, cot).astype(BF)
     act_grad = dot_tb(cot, full_down)
     gate_grad = act_grad * up_val * sig_g * (1.0 + gate_val * (1.0 - sig_g))
     up_grad = act_grad * gate_val * sig_g
     gu_grad = jnp.concatenate([gate_grad.astype(BF), up_grad.astype(BF)], axis=1)
-    gu_w = scatter_all(dot_ta(normed_two, gu_grad))
+    gu_w = dot_ta(normed_two, gu_grad).astype(BF)
     normed_two_grad = dot_tb(gu_grad, full_gu)
     two_grad = jnp.sum(resid * scale_two * normed_two_grad, axis=0)
     resid_grad = cot.astype(F32) + norm_back(resid, scale_two, gain_two, normed_two_grad)
@@ -482,8 +489,14 @@
         scatter_dimension=0,
         tiled=True,
     )
-    mixer_w = scatter_all(dot_ta(mixed, resid_low))
-    attn_w = scatter_all(dot_ta(attn_mix, resid_low))
+    mixer_w = dot_ta(mixed, resid_low).astype(BF)
+    attn_w = dot_ta(attn_mix, resid_low).astype(BF)
+    tall_w = scatter_all(
+        jnp.concatenate(
+            [w.reshape(owners, -1, w.shape[1]) for w in (down_w, mixer_w, attn_w)], axis=1
+        ).reshape(owners * rows_at[3], -1)
+    )
+    down_w, mixer_w, attn_w = [tall_w[rows_at[i] : rows_at[i + 1]] for i in range(3)]
 
     inner_x, gram_grad, row_sum, col_sum = inner_backward(
         x_low, out_low, gram, log_decay, log_row, dt_row, seg_col, seg_row
@@ -530,10 +543,10 @@
             query_grad,
             kv_grad,
             raw_grad.astype(BF),
+            jnp.zeros((t, extra), BF),
         ],
         axis=1,
     )
-    pack_w = scatter_all(dot_ta(normed, pack_grad))
     normed_grad = dot_tb(pack_grad, in_pack)
     one_grad = jnp.sum(hidden * scale_one * normed_grad, axis=0)
     input_grad = resid_grad + norm_back(hidden, scale_one, gain_one, normed_grad)
@@ -548,13 +561,20 @@
         ],
         axis=1,
     )
-    small_own = scatter_all(small_grad)[0]
+    small_grad = jnp.pad(small_grad, ((0, 0), (0, extra * own_d - n_small)))
+    pack_w = dot_ta(normed, pack_grad) + jnp.pad(
+        small_grad.reshape(width, extra), ((0, 0), (PACK, 0))
+    )
+    pack_w = pack_w.astype(BF)
+    wide_w = scatter_all(jnp.concatenate([gu_w, pack_w], axis=1))
+    gu_w, pack_w = wide_w[:, : 2 * ff], wide_w[:, 2 * ff :]
+    small_own = pack_w[:, PACK:].reshape(-1)
     head_sums = lax.psum(jnp.stack([step_bias_grad, decay_log_grad, skip_grad]), BOTH)
     taps_cut = CONV * own_conv
     return (
         layer_out[None],
         input_grad[None],
-        jnp.concatenate([pack_w[:, :Q_AT], pack_w[:, RAW_AT:]], axis=1),
+        jnp.concatenate([pack_w[:, :Q_AT], pack_w[:, RAW_AT:PACK]], axis=1),
         pack_w[:, Q_AT:K_AT],
         pack_w[:, K_AT:V_AT],
         pack_w[:, V_AT:RAW_AT],
@@ -567,7 +587,7 @@
         small_own[taps_cut:cut],
         small_own[cut : cut + own_d],
         small_own[cut + own_d : cut + 2 * own_d],
-        small_own[cut + 2 * own_d :],
+        small_own[cut + 2 * own_d : n_small],
         head_sums[0],
         head_sums[1],
         head_sums[2],

time: 1150 us -> 718 us (0.62)
  waiting for transfers between devices: 762 us -> 335 us
  blocking collectives: 132 us -> 60.9 us
  local copies, waits for them, and re-layouts: 47.2 us -> 106 us
  other arithmetic: 49.1 us -> 70.9 us
  matrix products: 99.3 us -> 81.6 us
    reduce_scatter x5 -> x1, waiting for transfers between devices: 509 us -> 0.01 us  [scatter_all(): lax.psum_scatter(a.astype(BF), BOTH, scatter_dimension=0, tiled=True)]
    unnamed x13 -> x9, waiting for transfers between devices: 1.89 us -> 168 us
    all_gather x5 -> x3, waiting for transfers between devices: 252 us -> 167 us  [gather_all(): return lax.all_gather(a, BOTH, axis=0, tiled=True)]
    unnamed x2 -> x0, blocking collectives: 83.8 us -> none
    concatenate x1 -> x4, other arithmetic: 0.79 us -> 28.6 us  [the longest x1 19.2 us: body(): wide_w = scatter_all(jnp.concatenate([gu_w, pack_w], axis=1))]
    slice x2 -> x14, local copies, waits for them, and re-layouts: 1.28 us -> 20.9 us  [the longest x3 11.5 us: body(): tall[:, rows_at[i]:rows_at[i + 1]].reshape(owners * own_rows[i], -1)]
    unnamed x276 -> x269, local copies, waits for them, and re-layouts: 21 us -> 40.4 us
    convert_element_type x1 -> x2, local copies, waits for them, and re-layouts: 0.08 us -> 12.2 us  [the longest x1 12.1 us: body(): gu_w = dot_ta(normed_two, gu_grad).astype(BF)]
  transfers between devices with their start and end apart: 15 -> 10, of which waited for: 10 -> 4; matrix products, arithmetic and copies ran while one was open for 12% -> 28% of each run, Pallas kernels for 3% -> 4%
where the time goes in v2:
time: 718 us; the launch traced here: 706 us
  waiting for transfers between devices  335 us (47%)
  local copies, waits for them, and re-layouts  106 us (15%)
  matrix products  81.6 us (11%)
  other arithmetic  70.9 us (10%)
  blocking collectives  60.9 us (8%)
  Pallas kernels  30.2 us (4%)
  between operations  17.3 us (2%)
    unnamed x9, waiting for transfers between devices  168 us
    all_gather x3, waiting for transfers between devices, gather_all(): return lax.all_gather(a, BOTH, axis=0, tiled=True)  167 us
    psum x1, blocking collectives, body(): lax.psum(jnp.stack([step_bias_grad, decay_log_grad, skip_grad]), BOTH)  42.5 us
    unnamed x269, local copies, waits for them, and re-layouts  40.4 us
    dot_general x8, matrix products, dot_ta(): lax.dot_general(a, b, (((0,), (0,)), ((), ())), preferred_element_type=F32)  26.1 us
    dot_general x8, matrix products, dot_tb(): lax.dot_general(a, b, (((1,), (1,)), ((), ())), preferred_element_type=F32)  24.7 us
    dot_general x8, matrix products, dot(): return jnp.dot(a, b, preferred_element_type=F32)  21.8 us
    concatenate x1, other arithmetic, body(): wide_w = scatter_all(jnp.concatenate([gu_w, pack_w], axis=1))  19.2 us
  transfers between devices with their start and end apart: 10, of which 4 were waited for; matrix products, arithmetic and copies ran while one was open for 28% of the time, Pallas kernels for 4%

profile of v2, /device:TPU:0, one launch (start us, length us, event | category | flops | bytes accessed | tf_op | source)
XLA Modules:
  0.0 705.9 jit_solution(1414891438727436282)
XLA Ops:
  21.0 74.4 %all-gather.7.cloned.1.call-done = bf16[1024,4133]{1,0:T(8,128)(2,1)} async-done(((bf16[32,4133]{1,0:T(8,128)(2,1)}), bf16[1024,4133]{1,0:T(8,128)(2,1)}) %all-gather.7.cloned.1.call-update) | async-done | bytes 8464400 | tf_op jit(solution)/shard_map/all_gather | solution.py:50
  98.5 6.0 convolution_convert_fusion.1
  109.5 4.4 fusion.82
  124.1 51.0 %all-gather.11.cloned.1.call-done = bf16[4096,1024]{1,0:T(8,128)(2,1)} async-done(((bf16[128,1024]{1,0:T(8,128)(2,1)}), bf16[4096,1024]{1,0:T(8,128)(2,1)}) %all-gather.11.cloned.1.call-update) | async-done | bytes 8388624 | tf_op jit(solution)/shard_map/all_gather | solution.py:50
  177.4 4.0 slice.445
  181.4 5.2 slice.458
  186.9 18.4 %all_gather.25 = bf16[1024,256]{1,0:T(8,128)(2,1)S(1)} all-gather(bf16[256,256]{1,0:T(8,128)(2,1)S(1)} %slice.447), channel_id=1, replica_groups=mesh['dp'=8,'seq'=4] {'seq'}, dimensions={0}, use_global_device_ids=true | all-gather | bytes 655360 | tf_op jit(solution)/shard_map/all_gather | solution.py:393
  206.3 6.2 shard_map.340
  216.0 5.5 shard_map.339
  228.1 4.3 multiply_reduce_fusion.7
  234.8 41.4 %all-gather.13.cloned.1.call-done = bf16[1024,4096]{1,0:T(8,128)(2,1)} async-done(((bf16[32,4096]{1,0:T(8,128)(2,1)}), bf16[1024,4096]{1,0:T(8,128)(2,1)}) %all-gather.13.cloned.1.call-update) | async-done | bytes 8388624 | tf_op jit(solution)/shard_map/all_gather | solution.py:50
  276.3 5.9 fusion.112
  282.2 3.8 multiply_convert_fusion.1
  286.0 4.9 multiply_reduce_fusion.8
  294.6 4.1 multiply_reduce_fusion.4
  305.7 9.9 %shard_map.342 = (bf16[256,512]{1,0:T(8,128)(2,1)S(1)}, f32[1024,256]{1,0:T(8,128)S(1)}, f32[1024,256]{1,0:T(8,128)S(1)}) custom-call(bf16[256,512]{1,0:T(8,128)(2,1)S(1)} %copy-done.9, bf16[1024,256]{1,0:T(8,128)(2,1)S(1)} %copy-done.1, bf16[1024,256]{1,0:T(8,128)(2,1)S(1)} %copy-done.3, bf16[256,512]{1,0:T(8,128)(2,1)S(1)} %convolution_convert_fusion.7.dm_ref, ...), custom_call_target="tpu_custom_call" | custom-call | flops 2684354560 | bytes 4194304 | tf_op jit(solution)/shard_map/pallas_call | solution.py:258
  317.6 3.9 convolution_convert_fusion.2
  321.5 3.4 convolution_convert_fusion.3
  325.4 6.9 pad_maximum_fusion.1
  339.3 8.5 %shard_map.341 = (f32[256,1536]{1,0:T(8,128)S(1)}, f32[256,256]{1,0:T(8,128)S(1)}, f32[256,24]{1,0:T(8,128)S(1)}, f32[24,256]{1,0:T(8,128)S(1)}) custom-call(bf16[256,1536]{1,0:T(8,128)(2,1)S(1)} %slice.626.x_ref, bf16[256,1536]{1,0:T(8,128)(2,1)S(1)} %get-tuple-element.184.dy_ref, f32[256,256]{1,0:T(8,128)S(1)} %copy-done.7, f32[256,24]{1,0:T(8,128)S(1)} %copy.172.log_ref, ...), custom_call_target="tpu_custom_call" | custom-call | flops 805306368 | bytes 3145728 | tf_op jit(solution)/shard_map/pallas_call | solution.py:151
  350.6 7.7 %convolution_convert_fusion = bf16[1024,4096]{1,0:T(8,128)(2,1)} fusion(bf16[256,2048]{1,0:T(8,128)(2,1)} %get-tuple-element.168, bf16[256,2048]{1,0:T(8,128)(2,1)} %get-tuple-element.167, f32[256,1024]{1,0:T(8,128)} %copy-done.36, f32[1024]{0:T(1024)S(1)} %copy-done.72, f32[256]{0:T(256)} %copy-done.99), kind=kOutput, calls=%fused_computation.3 | convolution fusion | flops 2156658688 | bytes 11539456 | tf_op jit(solution)/shard_map/dot_general | solution.py:38
  358.3 12.1 %copy.195 = bf16[1024,4096]{0,1:T(8,128)(2,1)} copy(bf16[1024,4096]{1,0:T(8,128)(2,1)} %convolution_convert_fusion) | data formatting | bytes 16777216 | tf_op jit(solution)/shard_map/convert_element_type | solution.py:468
  374.2 4.5 fusion.36
  381.5 2.8 fusion.46
  399.0 4.2 concatenate.88
  403.2 7.7 %fusion.20 = (f32[1024]{0:T(1024)S(1)}, f32[256]{0:T(256)S(1)}, f32[256,1024]{1,0:T(8,128)}) fusion(bf16[1,256,1024]{2,1,0:T(8,128)(2,1)S(1)} %copy-done.53, f32[256]{0:T(256)S(1)} %copy-done.112, f32[1024]{0:T(1024)S(1)} %copy-done.103, bf16[256,4133]{1,0:T(8,128)(2,1)} %concatenate.88, bf16[1024,4133]{1,0:T(8,128)(2,1)} %all-gather.7.cloned.1.call-done), kind=kOutput, calls=%fused_computation.73 | convolution fusion | flops 2168716032 | bytes 12163584 | tf_op jit(solution)/shard_map/dot_general | solution.py:42
  412.0 6.5 add_convert_fusion
  418.6 19.2 %pad_maximum_fusion = bf16[1024,8229]{0,1:T(8,128)(2,1)} fusion(bf16[1024,4133]{0,1:T(8,128)(2,1)} %add_convert_fusion, bf16[1024,4096]{0,1:T(8,128)(2,1)} %copy.195), kind=kLoop, calls=%fused_computation.1 | loop fusion | flops 33705984 | bytes 33705984 | tf_op jit(solution)/shard_map/concatenate | solution.py:569
  437.8 21.4 %copy.213 = bf16[1024,8229]{1,0:T(8,128)(2,1)} copy(bf16[1024,8229]{0,1:T(8,128)(2,1)} %pad_maximum_fusion) | data formatting | bytes 33705984
  460.4 4.7 fusion.18
  465.1 42.5 %psum.7 = f32[3,24]{1,0:T(4,128)S(1)} all-reduce(f32[3,24]{1,0:T(4,128)S(1)} %pad_maximum_fusion.12), channel_id=1, replica_groups=mesh['dp'=8,'seq'=4] {'dp','seq'}, use_global_device_ids=true, to_apply=%region_24.25 | all-reduce | flops 72 | bytes 576 | tf_op jit(solution)/shard_map/psum | solution.py:572
  515.2 167.8 %reduce-scatter.10.cloned.1.call-done = bf16[32,8229]{1,0:T(8,128)(2,1)} async-done(((bf16[1024,8229]{1,0:T(8,128)(2,1)}), bf16[32,8229]{1,0:T(8,128)(2,1)}) %reduce-scatter.10.cloned.1.call-update) | async-done | bytes 526672
  (447 shorter events, 115.3 us)
Async XLA Ops:
  7.2 11.1 %copy-start.51 = (bf16[1,256,1024]{2,1,0:T(8,128)(2,1)S(1)}, bf16[1,256,1024]{2,1,0:T(8,128)(2,1)}, u32[]{:S(2)}) copy-start(bf16[1,256,1024]{2,1,0:T(8,128)(2,1)} %param.20) | copy-start | bytes 1572868
  7.2 11.3 %copy-start.125 = (f32[24]{0:T(128)S(1)}, f32[24]{0:T(128)}, u32[]{:S(2)}) copy-start(f32[24]{0:T(128)} %param.38) | copy-start | bytes 292
  7.2 88.2 %all-gather.7.cloned.1.call-start = ((), (), s32[]{:S(2)}) async-start(), calls=%async_computation.3 | async-start | bytes 8921088 | tf_op jit(solution)/shard_map/all_gather | solution.py:50
  14.2 160.9 %all-gather.11.cloned.1.call-start = ((), (), s32[]{:S(2)}) async-start(), calls=%async_computation.5 | async-start | bytes 8650752 | tf_op jit(solution)/shard_map/all_gather | solution.py:50
  16.0 205.5 %all-gather.9.cloned.1.call-start = ((), (), s32[]{:S(2)}) async-start(), calls=%async_computation.4 | async-start | bytes 1986560 | tf_op jit(solution)/shard_map/all_gather | solution.py:421
  18.3 91.2 %copy-start.64 = (f32[24,1536]{1,0:T(8,128)}, f32[24,1536]{1,0:T(8,128)S(1)}, u32[]{:S(2)}) copy-start(f32[24,1536]{1,0:T(8,128)S(1)} %reshape.411) | copy-start | bytes 442372
  18.5 88.3 %copy-start.127 = (f32[24]{0:T(128)}, f32[24]{0:T(128)S(1)}, u32[]{:S(2)}) copy-start(f32[24]{0:T(128)S(1)} %exponential_negate_fusion) | copy-start | bytes 292
  19.1 85.5 %copy-start.111 = (f32[256]{0:T(256)}, f32[256]{0:T(256)S(1)}, u32[]{:S(2)}) copy-start(f32[256]{0:T(256)S(1)} %get-tuple-element.218) | copy-start | bytes 3076
  21.0 86.3 %copy-start.113 = (f32[256]{0:T(256)}, f32[256]{0:T(256)S(1)}, u32[]{:S(2)}) copy-start(f32[256]{0:T(256)S(1)} %get-tuple-element.210) | copy-start | bytes 3076
  21.0 95.7 %copy-start.104 = (f32[256]{0:T(256)}, f32[256]{0:T(256)S(1)}, u32[]{:S(2)}) copy-start(f32[256]{0:T(256)S(1)} %get-tuple-element.212) | copy-start | bytes 3076
  104.6 82.0 %copy-start.57 = (bf16[256,4133]{1,0:T(8,128)(2,1)}, bf16[256,4133]{1,0:T(8,128)(2,1)S(1)}, u32[]{:S(2)}) copy-start(bf16[256,4133]{1,0:T(8,128)(2,1)S(1)} %convolution_convert_fusion.1) | copy-start | bytes 6348292
  104.6 10.7 %collective-permute-start = (bf16[3,1792]{1,0:T(4,128)(2,1)S(1)}, bf16[3,1792]{1,0:T(4,128)(2,1)S(1)}, u32[]{:S(2)}, u32[]{:S(2)}) collective-permute-start(bf16[3,1792]{1,0:T(4,128)(2,1)S(1)} %slice.419), channel_id=1, source_target_pairs={{0,1},{1,2},{2,3},{4,5},{5,6},{6,7},{8,9},{9,10},{10,11},{12,13},{... | collective-permute-start | bytes 32264 | tf_op jit(solution)/shard_map/ppermute | solution.py:392
  107.2 108.8 %copy-start.13 = (f32[256,24]{0,1:T(8,128)}, f32[256,24]{0,1:T(8,128)S(1)}, u32[]{:S(2)}) copy-start(f32[256,24]{0,1:T(8,128)S(1)} %fusion.55) | copy-start | bytes 73732
  122.8 153.4 %all-gather.13.cloned.1.call-start = ((), (), s32[]{:S(2)}) async-start(), calls=%async_computation.6 | async-start | bytes 8650752 | tf_op jit(solution)/shard_map/all_gather | solution.py:50
  123.6 250.6 %all-gather.15.cloned.1.call-start = ((), (), s32[]{:S(2)}) async-start(), calls=%async_computation.9 | async-start | bytes 1966080 | tf_op jit(solution)/shard_map/all_gather | solution.py:483
  123.9 104.1 %copy-start.94 = (f32[1536]{0:T(1024)}, f32[1536]{0:T(1024)S(1)}, u32[]{:S(2)}) copy-start(f32[1536]{0:T(1024)S(1)} %mul.729) | copy-start | bytes 18436
  124.1 91.9 %copy-start.10 = (s32[256,1]{1,0:T(8,128)}, s32[256,1]{1,0:T(8,128)S(1)}, u32[]{:S(2)}) copy-start(s32[256,1]{1,0:T(8,128)S(1)} %copy.174.sc_ref) | copy-start | bytes 3076
  186.6 19.7 %copy-start.8 = (bf16[256,512]{1,0:T(8,128)(2,1)}, bf16[256,512]{1,0:T(8,128)(2,1)S(1)}, u32[]{:S(2)}) copy-start(bf16[256,512]{1,0:T(8,128)(2,1)S(1)} %slice.446.q_ref) | copy-start | bytes 786436
  186.9 104.0 %copy-start.71 = (f32[1024]{0:T(1024)}, f32[1024]{0:T(1024)S(1)}, u32[]{:S(2)}) copy-start(f32[1024]{0:T(1024)S(1)} %mul.742) | copy-start | bytes 12292
  186.9 29.0 %copy-start.15 = (f32[24,256]{1,0:T(8,128)}, f32[24,256]{1,0:T(8,128)S(1)}, u32[]{:S(2)}) copy-start(f32[24,256]{1,0:T(8,128)S(1)} %copy.173.dt_row_ref) | copy-start | bytes 73732
  232.4 62.2 %copy-start.76 = (f32[256]{0:T(256)}, f32[256]{0:T(256)S(1)}, u32[]{:S(2)}) copy-start(f32[256]{0:T(256)S(1)} %get-tuple-element.220) | copy-start | bytes 3076
  234.8 56.1 %copy-start.36 = (f32[256,1024]{1,0:T(8,128)}, f32[256,1024]{1,0:T(8,128)S(1)}, u32[]{:S(2)}) copy-start(f32[256,1024]{1,0:T(8,128)S(1)} %get-tuple-element.224) | copy-start | bytes 3145732
  234.8 56.1 %copy-start.99 = (f32[256]{0:T(256)}, f32[256]{0:T(256)S(1)}, u32[]{:S(2)}) copy-start(f32[256]{0:T(256)S(1)} %get-tuple-element.222) | copy-start | bytes 3076
  303.7 95.3 %reduce-scatter.6.cloned.1.call-start = ((), (), s32[]{:S(2)}) async-start(), calls=%async_computation.7 | async-start | bytes 655360 | tf_op jit(solution)/shard_map/reduce_scatter | solution.py:486
  324.9 185.8 %reduce-scatter.8.cloned.1.call-start = ((), (), s32[]{:S(2)}) async-start(), calls=%async_computation.8 | async-start | bytes 8650752 | tf_op jit(solution)/shard_map/reduce_scatter | solution.py:54
  332.3 18.2 %copy-start.72 = (f32[1024]{0:T(1024)S(1)}, f32[1024]{0:T(1024)}, u32[]{:S(2)}) copy-start(f32[1024]{0:T(1024)} %copy-done.71) | copy-start | bytes 12292
  332.4 350.6 %reduce-scatter.10.cloned.1.call-start = ((), (), s32[]{:S(2)}) async-start(), calls=%async_computation.10 | async-start | bytes 17571840
  358.3 14.9 %copy-start.48 = (bf16[256,1536]{1,0:T(8,128)(2,1)S(1)}, bf16[256,1536]{1,0:T(8,128)(2,1)}, u32[]{:S(2)}) copy-start(bf16[256,1536]{1,0:T(8,128)(2,1)} %copy-done.47) | copy-start | bytes 2359300
  358.3 14.9 %copy-start.59 = (bf16[1536,128]{1,0:T(8,128)(2,1)S(1)}, bf16[1536,128]{1,0:T(8,128)(2,1)}, u32[]{:S(2)}) copy-start(bf16[1536,128]{1,0:T(8,128)(2,1)} %copy-done.58) | copy-start | bytes 1179652
  391.3 7.5 %collective-permute-start.1 = (f32[3,1792]{1,0:T(4,128)S(1)}, f32[3,1792]{1,0:T(4,128)S(1)}, u32[]{:S(2)}, u32[]{:S(2)}) collective-permute-start(f32[3,1792]{1,0:T(4,128)S(1)} %pad_add_fusion.1), channel_id=1, source_target_pairs={{1,0},{2,1},{3,2},{5,4},{6,5},{7,6},{9,8},{10,9},{11,10},{13,12},{... | collective-permute-start | bytes 64520 | tf_op jit(solution)/shard_map/ppermute | solution.py:537
  460.4 47.7 %copy-start.54 = (f32[256,1024]{1,0:T(8,128)S(1)}, f32[256,1024]{1,0:T(8,128)}, u32[]{:S(2)}) copy-start(f32[256,1024]{1,0:T(8,128)} %get-tuple-element.158) | copy-start | bytes 3145732
  460.4 47.7 %copy-start.110 = (f32[256]{0:T(256)S(1)}, f32[256]{0:T(256)}, u32[]{:S(2)}) copy-start(f32[256]{0:T(256)} %get-tuple-element.217) | copy-start | bytes 3076
  (109 other events, 351.7 us)
Sparse Core Ops, SparseCore 0:
  14.3 81.0 all-gather.6
  98.9 76.1 all-gather.10
  177.2 18.3 all-gather.8
  198.9 77.3 all-gather.12
  303.8 18.2 all-gather.14
  325.0 21.7 reduce-scatter.5
  349.2 149.0 reduce-scatter.7
  500.6 182.3 reduce-scatter.9
